TPU v7x, 32 devices: a whole 2x2x4 slice. The times are simulated.
32 devices in a mesh: dp: 4 (over y, core), seq: 8 (over z, x).
Axes of the slice: x: 2, y: 2, z: 4, core: 2. Of those that a mesh axis runs over, the one named last changes fastest.
Arguments:
- features: bfloat16 [4, 6144, 512], P('dp', 'seq'), may hold values from -12 to 12, as said below
- slot_kind: int32 [4, 24], P('dp', 'seq'), may hold values from 0 to 2, as said below
- block_gain: float32 [512], replicated, may hold values from 0.1 to 1.9
- block_shift: float32 [512], replicated, may hold values from -2 to 2
- block_weight: bfloat16 [4608, 512], replicated, may hold values from -0.09375 to 0.09375
- block_bias: float32 [512], replicated, may hold values from -2 to 2
- final_gain: float32 [512], replicated, may hold values from 0.1 to 1.9
- final_shift: float32 [512], replicated, may hold values from -2 to 2
- latent_weight: bfloat16 [512, 144], replicated, may hold values from -0.09375 to 0.09375
- latent_bias: float32 [16], replicated, may hold values from -2 to 2
- embed_weight: bfloat16 [64, 1152], P(None, 'dp'), may hold values from -0.75 to 0.75
- embed_bias: bfloat16 [1152], P('dp'), may hold values from -2 to 2
Outputs:
- sequence: bfloat16 [4, 1024, 1152], P('dp', 'seq')
Inputs may be any that keep to these rules, and one draw needn't show every extreme that they name: `slot_kind`: the live slots of a device (kind 1 or 2) come before its empty ones. In every dp group, the live slots of the devices with seq index below d number between 2 d and 2 d + 2, and 2 * 8 over the whole group; in every group some device has 3 live slots. `features`: finite values.
All inputs are finite; a program needn't handle non-finite values.
Results may differ from a plain program's by a relative error of at most 0.014.
Values may be sent and summed in bfloat16 or wider, within the bound.
No kernel may reach another device: no remote copies, remote signals or barrier semaphores. Data moves between devices by JAX's collectives and lax.ppermute only.
A program may use at most 64 MiB of HBM per device.

v0:
```python
import functools
import jax
import jax.numpy as jnp
from jax import lax
from jax.sharding import PartitionSpec as P
from jax.sharding import PartitionSpec as P
from jax.experimental import pallas as pl
from jax.experimental.pallas import tpu as pltpu

GROUPS = 32
SLOT_ROWS = 32
SLOT_COLS = 8
LATENT_SHIFT = 0.0609
LATENT_SCALE = 1.5305
NORM_EPSILON = 1e-06
LANES = 128
ROW_STEPS = (0, -1, 1)
VMEM_BYTES = 64 * 1024 * 1024
F32 = jnp.float32
BF16 = jnp.bfloat16


def group_total(stats, same_group):
    rows, channels = stats.shape
    chunks = channels // LANES
    packed = jnp.concatenate([stats[:, k * LANES:(k + 1) * LANES] for k in range(chunks)], axis=0)
    high = packed.astype(BF16)
    rest = packed - high.astype(F32)
    middle = rest.astype(BF16)
    low = (rest - middle.astype(F32)).astype(BF16)
    total = sum(jnp.dot(piece, same_group, preferred_element_type=F32) for piece in (high, middle, low))
    return jnp.concatenate([total[k * rows:(k + 1) * rows] for k in range(chunks)], axis=1)


def affine(stats, joined, gain, shift, same_group, count):
    total = group_total(stats, same_group)
    mean, square = total[0:2] * (1.0 / count), total[2:4] * (1.0 / count)
    both_mean = 0.5 * (mean[0:1] + mean[1:2])
    both_square = 0.5 * (square[0:1] + square[1:2])
    mean = jnp.where(joined, both_mean, mean)
    square = jnp.where(joined, both_square, square)
    spread = jnp.maximum(square - mean * mean, 0.0)
    scale = lax.rsqrt(spread + NORM_EPSILON) * (0.5 * gain)
    return scale, 0.5 * shift - mean * scale


def half_stats(half):
    total = jnp.sum(half, axis=0, keepdims=True)
    return total, jnp.sum(half * half, axis=0, keepdims=True)


def norm_first_steps(x_ref, joined, gain, shift, same_group, z_ref, u_ref):
    cells, channels = x_ref.shape
    half = cells // 2
    rows = cells // SLOT_COLS
    chunks = channels // LANES
    count = half * (channels // GROUPS)
    keep = jnp.where(joined, 1.0, 0.0).astype(F32)
    column = lax.broadcasted_iota(jnp.int32, (1, SLOT_COLS, 1), 1)
    parts = []
    for k in range(chunks):
        x = x_ref[:, k * LANES:(k + 1) * LANES].astype(F32)
        t0, q0 = half_stats(x[:half])
        t1, q1 = half_stats(x[half:])
        parts.append(jnp.concatenate([t0, t1, q0, q1], axis=0))
        yield
    scale, offset = affine(jnp.concatenate(parts, axis=1), joined, gain, shift, same_group, count)
    zero = jnp.zeros((SLOT_COLS, LANES), F32)
    for k in range(chunks):
        lanes = slice(k * LANES, (k + 1) * LANES)
        x = x_ref[:, lanes].astype(F32)
        v = jnp.concatenate([x[:half] * scale[0:1, lanes] + offset[0:1, lanes],
                             x[half:] * scale[1:2, lanes] + offset[1:2, lanes]], axis=0)
        act = v + v * jnp.tanh(v)
        act3 = act.reshape(rows, SLOT_COLS, LANES)
        left = jnp.where(column == 0, 0.0, pltpu.roll(act3, 1, 1)).reshape(cells, LANES)
        right = jnp.where(column == SLOT_COLS - 1, 0.0, pltpu.roll(act3, SLOT_COLS - 1, 1)).reshape(cells, LANES)
        for b, value in enumerate((left, act, right)):
            z_ref[b, :, lanes] = value.astype(BF16)
            over = value[half:half + SLOT_COLS] * keep
            under = value[half - SLOT_COLS:half] * keep
            u_ref[b, 0, :, lanes] = jnp.concatenate([zero, value[:half], over], axis=0).astype(BF16)
            u_ref[b, 1, :, lanes] = jnp.concatenate([under, value[half:], zero], axis=0).astype(BF16)
        yield


def conv_steps(x_ref, bias, wbuf, wait_weights, z_ref, u_ref, y_ref):
    cells, channels = x_ref.shape
    half = cells // 2
    tile = channels // 2
    totals = [x_ref[:, k * tile:(k + 1) * tile].astype(F32) + bias[:, k * tile:(k + 1) * tile] for k in range(2)]
    for step, a in enumerate(ROW_STEPS):
        wait_weights(step)
        for b in range(3):
            if a == 0:
                lhs = z_ref[b]
            else:
                first = 0 if a < 0 else 2 * SLOT_COLS
                lhs = jnp.concatenate([u_ref[b, h, first:first + half, :] for h in range(2)], axis=0)
            base = (3 * (a + 1) + b) * channels
            for k in range(2):
                totals[k] = totals[k] + jnp.dot(lhs, wbuf[base:base + channels, k * tile:(k + 1) * tile],
                                                preferred_element_type=F32)
                yield
    for k in range(2):
        y_ref[:, k * tile:(k + 1) * tile] = totals[k].astype(BF16)
    yield


def drain(steps):
    for _ in steps:
        pass


def interleave(main, *others):
    for _ in main:
        for steps in others:
            next(steps, None)
    for steps in others:
        drain(steps)


def norm_second_steps(y_ref, joined, gain, shift, same_group):
    cells, channels = y_ref.shape
    half = cells // 2
    chunks = channels // LANES
    count = half * (channels // GROUPS)
    parts = []
    for k in range(chunks):
        lanes = slice(k * LANES, (k + 1) * LANES)
        inner = y_ref[:, lanes].astype(F32)
        t0, q0 = half_stats(inner[:half])
        t1, q1 = half_stats(inner[half:])
        parts.append(jnp.concatenate([t0, t1, q0, q1], axis=0))
        yield
    scale, offset = affine(jnp.concatenate(parts, axis=1), joined, gain, shift, same_group, count)
    for k in range(chunks):
        lanes = slice(k * LANES, (k + 1) * LANES)
        y = y_ref[:, lanes].astype(F32)
        v = jnp.concatenate([y[:half] * scale[0:1, lanes] + offset[0:1, lanes],
                             y[half:] * scale[1:2, lanes] + offset[1:2, lanes]], axis=0)
        y_ref[:, lanes] = (v + v * jnp.tanh(v)).astype(BF16)
        yield


def to_patches_steps(store, y_ref, joined, table_ref, bias, gather):
    cells, channels = y_ref.shape
    rows = cells // SLOT_COLS
    mid = rows // 2
    tokens = gather.shape[0]
    lat = channels // GROUPS
    keep = jnp.where(joined, 1.0, 0.0).astype(F32)
    column = lax.broadcasted_iota(jnp.int32, (1, SLOT_COLS, 1), 1)
    block = whole(lax.broadcasted_iota(jnp.int32, (1, SLOT_COLS, LANES), 2), lat)
    taps = jnp.dot(y_ref[...], table_ref[...], preferred_element_type=F32)
    yield
    from_left, here, from_right = (taps[:, k * LANES:(k + 1) * LANES].reshape(rows, SLOT_COLS, LANES) for k in range(3))
    moved = here + jnp.where(column == 0, 0.0, pltpu.roll(from_left, 1, 1))
    moved = moved + jnp.where(column == SLOT_COLS - 1, 0.0, pltpu.roll(from_right, SLOT_COLS - 1, 1))
    yield
    blank = jnp.zeros((1, SLOT_COLS, LANES), F32)
    above = jnp.concatenate([blank, moved[:mid - 1], moved[mid - 1:mid] * keep, moved[mid:rows - 1]], axis=0)
    below = jnp.concatenate([moved[1:mid], moved[mid:mid + 1] * keep, moved[mid + 1:], blank], axis=0)
    step_up = (block == 0) | (block == 3)
    step_none = (block == 1) | (block == 4)
    mixed = jnp.where(step_up, above, jnp.where(step_none, moved, below)).reshape(cells, LANES)
    yield
    latent = mixed + pltpu.roll(mixed, LANES - lat, 1) + pltpu.roll(mixed, LANES - 2 * lat, 1)
    latent = ((latent + bias) - LATENT_SHIFT) * LATENT_SCALE
    corner = block - part(lax.broadcasted_iota(jnp.int32, (1, SLOT_COLS, LANES), 1), 2)
    corner = jnp.concatenate([corner, corner - 2], axis=0)
    latent = latent.reshape(rows // 2, 2, SLOT_COLS, LANES)
    latent = jnp.where((corner == 0)[None], latent, 0.0).reshape(cells, LANES)
    yield
    store(jnp.dot(gather, latent.astype(BF16), preferred_element_type=F32)[:, :4 * lat].astype(BF16))
    yield


def patch_tables(lw_ref, bias_ref, table_ref, bias4_ref):
    lat = lw_ref.shape[0] // 9
    weight = lw_ref[...].astype(F32)
    blank = jnp.zeros((2 * lat, weight.shape[1]), F32)
    for b in range(3):
        blocks = [weight[(3 * a + b) * lat:(3 * a + b + 1) * lat] for a in range(3)]
        table_ref[:, b * LANES:(b + 1) * LANES] = jnp.concatenate(blocks * 2 + [blank], axis=0).T.astype(BF16)
    bias4_ref[...] = jnp.concatenate([bias_ref[...].reshape(1, lat)] * (LANES // lat), axis=1)
    yield


def whole(value, size):
    return value >> (size.bit_length() - 1)


def part(value, size):
    return value & (size - 1)


def group_table(channels):
    width = channels // GROUPS
    r = whole(lax.broadcasted_iota(jnp.int32, (LANES, LANES), 0), width)
    c = whole(lax.broadcasted_iota(jnp.int32, (LANES, LANES), 1), width)
    return jnp.where(r == c, 1.0, 0.0).astype(BF16)


def patch_table(cells):
    half_cols = SLOT_COLS // 2
    token = lax.broadcasted_iota(jnp.int32, (cells // 4, cells), 0)
    cell = lax.broadcasted_iota(jnp.int32, (cells // 4, cells), 1)
    own = whole(whole(cell, SLOT_COLS), 2) * half_cols + whole(part(cell, SLOT_COLS), 2)
    return jnp.where(own == token, 1.0, 0.0).astype(BF16)


def finish_steps(store, y_ref, joined, gain, shift, same_group, table_ref, bias4, gather):
    yield from norm_second_steps(y_ref, joined, gain, shift, same_group)
    yield from to_patches_steps(store, y_ref, joined, table_ref, bias4, gather)


FIRST = 1


def vector(ref):
    return ref[...].reshape(1, ref.shape[0])


def load_kernel(kind_hbm, feat_hbm, ew_hbm, eb_hbm, *rest):
    names = 7
    small_hbm, rest = rest[:names], rest[names:]
    state_ref, x_ref, piece_ref, *rest = rest
    small, rest = rest[:names], rest[names:]
    kind_ref, ew_ref, eb_ref, ksem, xsem, ssem = rest
    slots = kind_ref.shape[1]
    cells = x_ref.shape[0]
    kcopy = pltpu.make_async_copy(kind_hbm, kind_ref, ksem)
    kcopy.start()
    xcopy = pltpu.make_async_copy(feat_hbm.at[0, pl.ds(FIRST * cells, cells), :], x_ref, xsem)
    scopies = [pltpu.make_async_copy(src, dst, ssem.at[i])
               for i, (src, dst) in enumerate(zip(small_hbm + (ew_hbm, eb_hbm), small + [ew_ref, eb_ref]))]
    for c in [xcopy] + scopies:
        c.start()
    kcopy.wait()
    live = jnp.int32(0)
    for s in range(slots):
        live = live + jnp.where(kind_ref[0, s] > 0, 1, 0).astype(jnp.int32)
        state_ref[2 + s] = kind_ref[0, s]
    state_ref[0] = live
    state_ref[1] = jnp.where(live > 2, 2, 0)
    for c in scopies:
        c.wait()
    feats = ew_ref.shape[0]
    piece_ref[0:feats, :] = ew_ref[...]
    piece_ref[feats:, :] = jnp.broadcast_to(vector(eb_ref), (piece_ref.shape[0] - feats, ew_ref.shape[1]))
    xcopy.wait()


def begin_kernel(state_ref, x_ref, gain_ref, shift_ref, lw_ref, lb_ref, piece_in,
                 z_ref, u_ref, table_ref, bias4_ref, perm_ref, piece_ref):
    piece_ref[...] = piece_in[...]
    perm_ref[...] = patch_table(x_ref.shape[0])
    interleave(norm_first_steps(x_ref, state_ref[2 + FIRST] == 2, vector(gain_ref), vector(shift_ref),
                                group_table(x_ref.shape[1]), z_ref, u_ref),
               patch_tables(lw_ref, lb_ref, table_ref, bias4_ref))


def second_norm(y_ref, kind, small):
    return norm_second_steps(y_ref, kind == 2, vector(small[3]), vector(small[4]), group_table(y_ref.shape[1]))


def patches(store, y_ref, kind, small, perm_ref):
    return to_patches_steps(store, y_ref, kind == 2, small[5], small[6][...], perm_ref[...])


def chain(*parts):
    for steps in parts:
        yield from steps


def count_live(kind_ref):
    total = jnp.int32(-2)
    for s in range(kind_ref.shape[1]):
        total = total + jnp.where(kind_ref[0, s] > 0, 1, 0).astype(jnp.int32)
    return total


def middle_kernel(offsets, state_ref, x_ref, w_ref, perm_ref, z_ref, u_ref, *rest):
    names = 7
    small, rest = rest[:names], rest[names:]
    others, rest = rest[:len(offsets)], rest[len(offsets):]
    message_ref, sums_ref, z3_ref, u3_ref, *rest = rest
    early_ref, y_ref, z2_ref, u2_ref, *rest = rest
    kinds, ksem = rest[:-1], rest[-1]
    copies = [pltpu.make_async_copy(src, dst, ksem.at[i]) for i, (src, dst) in enumerate(zip(others, kinds))]
    for c in copies:
        c.start()
    cells = early_ref.shape[0]
    tokens = cells // 4
    feats = message_ref.shape[1] // 2
    slot = state_ref[1]

    def features_of(at):
        return x_ref.at[0, pl.ds(pl.multiple_of(at * cells, cells), cells), :]

    def first_norm(at, z_to, u_to):
        return norm_first_steps(features_of(at), state_ref[2 + at] == 2, vector(small[0]), vector(small[1]),
                                group_table(x_ref.shape[2]), z_to, u_to)

    def encode_two(with_third):
        found = {}

        def keep_as(name):
            def store(value):
                found[name] = value
            return store

        kind, early_kind = state_ref[2 + slot], state_ref[2 + FIRST]
        third = [first_norm(0, z3_ref, u3_ref)] if with_third else []
        interleave(conv_steps(features_of(FIRST), vector(small[2]), w_ref, lambda step: None, z_ref, u_ref, early_ref),
                   first_norm(slot, z2_ref, u2_ref))
        interleave(conv_steps(features_of(slot), vector(small[2]), w_ref, lambda step: None, z2_ref, u2_ref, y_ref),
                   chain(second_norm(early_ref, early_kind, small), *third))
        interleave(chain(second_norm(y_ref, kind, small), patches(keep_as("second"), y_ref, kind, small, perm_ref)),
                   patches(keep_as("first"), early_ref, early_kind, small, perm_ref))
        first_is_last = state_ref[0] == 2
        last = jnp.where(first_is_last, found["first"], found["second"])
        before = jnp.where(first_is_last, found["second"], found["first"])
        message_ref[0:tokens, :] = jnp.concatenate([last, before], axis=1)

    pl.when(state_ref[0] > 2)(lambda: encode_two(True))
    pl.when(state_ref[0] <= 2)(lambda: encode_two(False))
    for c in copies:
        c.wait()
    position = lax.axis_index("seq")
    mine = state_ref[0] - 2
    below, above = jnp.int32(0), mine
    for offset, kind_ref in zip(offsets, kinds):
        other = count_live(kind_ref)
        lower = (position ^ offset) < position
        below = below + jnp.where(lower, other, 0)
        above = above + jnp.where(lower, 0, other)
    first_half = position < lax.axis_size("seq") // 2
    passed = jnp.where(position % 2 == 0, mine, 0)
    sums_ref[0] = jnp.where(first_half, below, -above)
    told = jnp.where(first_half, below + passed, passed - above)
    message_ref[tokens:, :] = jnp.full((message_ref.shape[0] - tokens, 2 * feats), told.astype(F32)).astype(BF16)


def final_kernel(parts, state_ref, x_ref, w_ref, perm_ref, z_ref, u_ref, *rest):
    pieces, small, rest = rest[:parts], rest[parts:parts + 7], rest[parts + 7:]
    out_ref, embed_ref, y_ref = rest
    group = lax.axis_index("dp")
    width = pieces[0].shape[1]

    def lay_out():
        for j in range(parts):
            value = pieces[0][...]
            for k in range(1, parts):
                value = jnp.where((group ^ j) == k, pieces[k][...], value)
            embed_ref[:, j * width:(j + 1) * width] = value
            yield

    @pl.when(state_ref[0] > 2)
    def _():
        def store(value):
            out_ref[...] = value

        interleave(conv_steps(x_ref.at[0, 0:y_ref.shape[0], :], vector(small[2]), w_ref, lambda step: None, z_ref, u_ref, y_ref),
                   lay_out())
        drain(second_norm(y_ref, state_ref[2], small))
        drain(patches(store, y_ref, state_ref[2], small, perm_ref))

    @pl.when(state_ref[0] <= 2)
    def _():
        drain(lay_out())
        out_ref[...] = jnp.zeros_like(out_ref)


def join_kernel(state_ref, sums_ref, own_ref, third_ref, even_ref, odd_ref, embed_ref, out_ref, source_ref, value_ref, sem):
    live = state_ref[0]
    odd = lax.axis_index("seq") % 2
    tokens, feats = third_ref.shape
    told = even_ref[tokens:, :].astype(F32)[0, 0].astype(jnp.int32)
    carry = sums_ref[0] + told
    for k, ref in enumerate((even_ref, odd_ref, own_ref)):
        source_ref[2 * k] = ref[0:tokens, 0:feats]
        source_ref[2 * k + 1] = ref[0:tokens, feats:]
    source_ref[6] = third_ref[...]
    weight = embed_ref[0:feats, :]
    bias = embed_ref[feats:feats + 1, :].astype(F32)
    copies = []
    for i in range(2):
        incoming = (1 - odd) * 2 + carry - 1 - i
        kept = 4 + live - 1 - (i - carry)
        patch = source_ref[jnp.clip(jnp.where(i < carry, incoming, kept), 0, 6)]
        value = jnp.dot(patch, weight, preferred_element_type=F32) + bias
        rows = pl.ds(i * tokens, tokens)
        value_ref[rows, :] = value.astype(BF16)
        copies.append(pltpu.make_async_copy(value_ref.at[rows, :], out_ref.at[0, rows, :], sem.at[i]))
        copies[i].start()
    for c in copies:
        c.wait()


def exchange(value, axis, offset):
    count = lax.axis_size(axis)
    return lax.ppermute(value, axis, [(i, i ^ offset) for i in range(count)])


def swap_odd_pairs(value):
    groups, count = lax.axis_size("dp"), lax.axis_size("seq")
    pairs = []
    for g in range(groups):
        pairs += [(g * count + end, (g ^ 1) * count + end) for end in (0, count - 1)]
        for i in range(1, count - 1, 2):
            pairs += [(g * count + i, g * count + i + 1), (g * count + i + 1, g * count + i)]
    return lax.ppermute(value, ("dp", "seq"), pairs)


VMEM_SPEC = pl.BlockSpec(memory_space=pltpu.VMEM)
SMEM_SPEC = pl.BlockSpec(memory_space=pltpu.SMEM)
ANY_SPEC = pl.BlockSpec(memory_space=pl.ANY)
MIB = 1024 * 1024


def cost(flops, moved):
    return pl.CostEstimate(flops=flops, bytes_accessed=moved, transcendentals=0)


def encode_flops(cells, channels, lat):
    return cells * channels * 2 * 9 * (channels + lat)


def load(features, slot_kind, embed_weight, embed_bias, small):
    channels = features.shape[2]
    cells = SLOT_ROWS * SLOT_COLS
    feats, width = embed_weight.shape
    return pl.pallas_call(
        load_kernel,
        out_shape=[
            pltpu.SMEM((8,), jnp.int32),
            pltpu.VMEM((cells, channels), BF16),
            pltpu.VMEM((feats + 16, width), BF16),
        ] + [pltpu.VMEM(v.shape, v.dtype) for v in small],
        in_specs=[ANY_SPEC] * (4 + len(small)),
        out_specs=[SMEM_SPEC] + [VMEM_SPEC] * (2 + len(small)),
        scratch_shapes=[
            pltpu.SMEM(slot_kind.shape, jnp.int32),
            pltpu.VMEM(embed_weight.shape, BF16),
            pltpu.VMEM(embed_bias.shape, BF16),
            pltpu.SemaphoreType.DMA,
            pltpu.SemaphoreType.DMA,
            pltpu.SemaphoreType.DMA((len(small) + 2,)),
        ],
        compiler_params=pltpu.CompilerParams(vmem_limit_bytes=63 * MIB),
        cost_estimate=cost(0, features.size),
        name="load",
    )(slot_kind, features, embed_weight, embed_bias, *small)


def local(features, slot_kind, block_gain, block_shift, block_weight, block_bias, final_gain, final_shift,
          latent_weight, latent_bias, embed_weight, embed_bias):
    seq, dp = lax.axis_size("seq"), lax.axis_size("dp")
    channels = features.shape[2]
    cells = SLOT_ROWS * SLOT_COLS
    tokens = cells // 4
    feats, width = embed_weight.shape
    small = (block_gain, block_shift, block_bias, final_gain, final_shift, latent_weight.T, latent_bias)
    offsets = tuple(range(2, seq // 2, 2))
    others = [exchange(slot_kind, "seq", offset) for offset in offsets]
    slot_buffer = pltpu.VMEM((cells, channels), BF16)
    flops = encode_flops(cells, channels, latent_bias.shape[0])
    state, x, piece, *small = load(features, slot_kind, embed_weight, embed_bias, small)
    z_buffer = pltpu.VMEM((3, cells, channels), BF16)
    u_buffer = pltpu.VMEM((3, 2, cells // 2 + 2 * SLOT_COLS, channels), BF16)
    z, u, table, bias4, perm, piece = pl.pallas_call(
        begin_kernel,
        out_shape=[z_buffer, u_buffer, pltpu.VMEM((channels, 3 * LANES), BF16), pltpu.VMEM((1, LANES), F32),
                   pltpu.VMEM((tokens, cells), BF16), pltpu.VMEM(piece.shape, BF16)],
        in_specs=[SMEM_SPEC] + [VMEM_SPEC] * 6,
        out_specs=[VMEM_SPEC] * 6,
        compiler_params=pltpu.CompilerParams(vmem_limit_bytes=16 * MIB),
        cost_estimate=cost(2 * flops, features.size),
        name="begin",
    )(state, x, *small[:2], *small[5:], piece)
    small = (*small[:5], table, bias4)
    message, sums, z3, u3 = pl.pallas_call(
        functools.partial(middle_kernel, offsets),
        out_shape=[jax.ShapeDtypeStruct((tokens + 16, 2 * feats), BF16), pltpu.SMEM((1,), jnp.int32), z_buffer, u_buffer],
        in_specs=[SMEM_SPEC] + [VMEM_SPEC] * (5 + len(small)) + [ANY_SPEC] * len(others),
        out_specs=[VMEM_SPEC, SMEM_SPEC] + [VMEM_SPEC] * 2,
        scratch_shapes=[slot_buffer] * 2 + [z_buffer, u_buffer] + [pltpu.SMEM(slot_kind.shape, jnp.int32) for _ in others]
        + [pltpu.SemaphoreType.DMA((len(others),))],
        compiler_params=pltpu.CompilerParams(vmem_limit_bytes=16 * MIB),
        cost_estimate=cost(flops, block_weight.size * 2),
        name="middle",
    )(state, features, block_weight, perm, z, u, *small, *others)
    even = exchange(message, "seq", 1)
    odd = swap_odd_pairs(message)
    pieces = [piece] + [exchange(piece, "dp", offset) for offset in range(1, dp)]
    third, embed = pl.pallas_call(
        functools.partial(final_kernel, dp),
        out_shape=[pltpu.VMEM((tokens, feats), BF16), pltpu.VMEM((feats + 16, dp * width), BF16)],
        in_specs=[SMEM_SPEC] + [VMEM_SPEC] * (5 + dp + len(small)),
        out_specs=[VMEM_SPEC] * 2,
        scratch_shapes=[slot_buffer],
        compiler_params=pltpu.CompilerParams(vmem_limit_bytes=16 * MIB),
        cost_estimate=cost(flops, block_weight.size * 2),
        name="final",
    )(state, features, block_weight, perm, z3, u3, *pieces, *small)
    return pl.pallas_call(
        join_kernel,
        out_shape=jax.ShapeDtypeStruct((1, 2 * tokens, dp * width), BF16),
        in_specs=[SMEM_SPEC] * 2 + [VMEM_SPEC] * 5,
        out_specs=ANY_SPEC,
        scratch_shapes=[pltpu.VMEM((7, tokens, feats), BF16), pltpu.VMEM((2 * tokens, dp * width), BF16),
                        pltpu.SemaphoreType.DMA((2,))],
        compiler_params=pltpu.CompilerParams(vmem_limit_bytes=8 * MIB),
        cost_estimate=cost(4 * tokens * feats * dp * width, 4 * tokens * dp * width),
        name="join",
    )(state, sums, message, third, even, odd, embed)


def solution(mesh):
    in_specs = (P("dp", "seq", None), P("dp", "seq")) + (P(),) * 8 + (P(None, "dp"), P("dp"))
    return jax.shard_map(local, mesh=mesh, in_specs=in_specs, out_specs=P("dp", "seq", None), check_vma=False)
```

profile of v0, /device:TPU:0, one launch (start us, length us, event | category | flops | bytes accessed | tf_op | source)
XLA Modules:
  0.0 16.2 jit_solution(4033414434053806844)
XLA Ops:
  0.0 3.0 %collective-permute-start = (s32[1,3]{1,0:T(1,128)}, s32[1,3]{1,0:T(1,128)S(1)}, u32[]{:S(2)}, u32[]{:S(2)}) collective-permute-start(s32[1,3]{1,0:T(1,128)} %kind_hbm.1), channel_id=1, source_target_pairs={{0,2},{1,3},{2,0},{3,1},{4,6},{5,7},{6,4},{7,5},{8,10},{9,11},{10,... | collective-permute-start | bytes 44 | tf_op jit(solution)/shard_map/ppermute | solution.py:404
  3.0 1.2 %load.1 = (s32[8]{0:T(128)S(4)}, bf16[256,512]{1,0:T(8,128)(2,1)S(1)}, bf16[80,288]{1,0:T(8,128)(2,1)S(1)}, f32[512]{0:T(512)S(1)}, f32[512]{0:T(512)S(1)}, /*in...) custom-call(s32[1,3]{1,0:T(1,128)} %kind_hbm.1, ...), custom_call_target="tpu_custom_call" | custom-call | bytes 393216 | tf_op jit(solution)/shard_map/load/pallas_call | solution.py:435
  4.2 0.0 slice-start
  4.2 0.0 copy-start
  4.2 0.0 slice-start.1
  4.2 0.7 %begin.1 = (bf16[3,256,512]{2,1,0:T(8,128)(2,1)S(1)}, bf16[3,2,144,512]{3,2,1,0:T(8,128)(2,1)S(1)}, bf16[512,384]{1,0:T(8,128)(2,1)S(1)}, f32[1,128]{1,0:T(1,128...) custom-call(s32[8]{0:T(128)S(4)} %get-tuple-element.27.state_ref, ...), custom_call_target="tpu_custom_call" | custom-call | flops 2491416576 | bytes 393216 | tf_op jit(solution)/shard_map/begin/pallas_call | solution.py:473
  4.9 0.7 %collective-permute-start.3 = (bf16[80,288]{1,0:T(8,128)(2,1)S(1)}, bf16[80,288]{1,0:T(8,128)(2,1)S(1)}, u32[]{:S(2)}, u32[]{:S(2)}) collective-permute-start(bf16[80,288]{1,0:T(8,128)(2,1)S(1)} %get-tuple-element.46.rest_0_), channel_id=1, source_target_pairs={{0,24},{8,16},{16,8},{24,0},{1,25},{9,17},{17,9},{25,1},{2,26},{10... | collective-permute-start | bytes 138248 | tf_op jit(solution)/shard_map/ppermute | solution.py:404
  5.7 0.9 %collective-permute-start.2 = (bf16[80,288]{1,0:T(8,128)(2,1)S(1)}, bf16[80,288]{1,0:T(8,128)(2,1)S(1)}, u32[]{:S(2)}, u32[]{:S(2)}) collective-permute-start(bf16[80,288]{1,0:T(8,128)(2,1)S(1)} %get-tuple-element.46.rest_0_), channel_id=1, source_target_pairs={{0,16},{8,24},{16,0},{24,8},{1,17},{9,25},{17,1},{25,9},{2,18},{10... | collective-permute-start | bytes 138248 | tf_op jit(solution)/shard_map/ppermute | solution.py:404
  6.6 0.3 %collective-permute-start.1 = (bf16[80,288]{1,0:T(8,128)(2,1)S(1)}, bf16[80,288]{1,0:T(8,128)(2,1)S(1)}, u32[]{:S(2)}, u32[]{:S(2)}) collective-permute-start(bf16[80,288]{1,0:T(8,128)(2,1)S(1)} %get-tuple-element.46.rest_0_), channel_id=1, source_target_pairs={{0,8},{8,0},{16,24},{24,16},{1,9},{9,1},{17,25},{25,17},{2,10},{10... | collective-permute-start | bytes 138248 | tf_op jit(solution)/shard_map/ppermute | solution.py:404
  6.9 0.0 collective-permute-done.rest_7_
  6.9 0.0 slice-done
  6.9 0.0 copy-done
  6.9 0.0 slice-done.1
  6.9 4.2 %middle.1 = (bf16[80,128]{1,0:T(8,128)(2,1)S(1)}, s32[1]{0:T(128)S(4)}, bf16[3,256,512]{2,1,0:T(8,128)(2,1)S(1)}, bf16[3,2,144,512]{3,2,1,0:T(8,128)(2,1)S(1)}) custom-call(s32[8]{0:T(128)S(4)} %get-tuple-element.27.state_ref, bf16[1,768,512]{2,1,0:T(8,128)(2,1)S(1)} %copy-done, bf16[4608,512]{1,0:T(8,128)(2,1)S(1)} %bitcast.2, ...), custom_call_target="tpu_custom_call" | custom-call | flops 1245708288 | bytes 4718592 | tf_op jit(solution)/shard_map/middle/pallas_call | solution.py:484
  11.1 0.3 %collective-permute-start.5 = (bf16[80,128]{1,0:T(8,128)(2,1)S(1)}, bf16[80,128]{1,0:T(8,128)(2,1)S(1)}, u32[]{:S(2)}, u32[]{:S(2)}) collective-permute-start(bf16[80,128]{1,0:T(8,128)(2,1)S(1)} %get-tuple-element.43.own_ref), channel_id=1, source_target_pairs={{0,8},{7,15},{1,2},{2,1},{3,4},{4,3},{5,6},{6,5},{8,0},{15,7},{9,1... | collective-permute-start | bytes 61448 | tf_op jit(solution)/shard_map/ppermute | solution.py:414
  11.4 1.1 %collective-permute-start.4 = (bf16[80,128]{1,0:T(8,128)(2,1)S(1)}, bf16[80,128]{1,0:T(8,128)(2,1)S(1)}, u32[]{:S(2)}, u32[]{:S(2)}) collective-permute-start(bf16[80,128]{1,0:T(8,128)(2,1)S(1)} %get-tuple-element.43.own_ref), channel_id=1, source_target_pairs={{0,1},{1,0},{2,3},{3,2},{4,5},{5,4},{6,7},{7,6},{8,9},{9,8},{10,11... | collective-permute-start | bytes 61448 | tf_op jit(solution)/shard_map/ppermute | solution.py:404
  12.5 0.0 collective-permute-done.3.rest_3_
  12.5 0.0 collective-permute-done.2.rest_2_
  12.5 0.0 collective-permute-done.1.rest_1_
  12.5 2.2 %final.1 = (bf16[64,64]{1,0:T(8,128)(2,1)S(1)}, bf16[80,1152]{1,0:T(8,128)(2,1)S(1)}) custom-call(s32[8]{0:T(128)S(4)} %get-tuple-element.27.state_ref, bf16[1,768,512]{2,1,0:T(8,128)(2,1)S(1)} %copy-done, bf16[4608,512]{1,0:T(8,128)(2,1)S(1)} %bitcast.2, bf16[64,256]{1,0:T(8,128)(2,1)S(1)} %get-tuple-element.34.perm_ref, ...), custom_call_target="tpu_custom_call" | custom-call | flops 1245708288 | bytes 4718592 | tf_op jit(solution)/shard_map/final/pallas_call | solution.py:498
  14.7 0.0 collective-permute-done.5.odd_ref
  14.7 0.5 %collective-permute-done.4.even_ref = bf16[80,128]{1,0:T(8,128)(2,1)S(1)} collective-permute-done((bf16[80,128]{1,0:T(8,128)(2,1)S(1)}, bf16[80,128]{1,0:T(8,128)(2,1)S(1)}, u32[]{:S(2)}, u32[]{:S(2)}) %collective-permute-start.4) | collective-permute-done | bytes 20512 | tf_op jit(solution)/shard_map/ppermute | solution.py:404
  15.2 1.0 %join.1 = bf16[1,128,1152]{2,1,0:T(8,128)(2,1)} custom-call(s32[8]{0:T(128)S(4)} %get-tuple-element.27.state_ref, s32[1]{0:T(128)S(4)} %get-tuple-element.42.sums_ref, bf16[80,128]{1,0:T(8,128)(2,1)S(1)} %get-tuple-element.43.own_ref, bf16[64,64]{1,0:T(8,128)(2,1)S(1)} %get-tuple-element.47.third_ref, bf16[80,128]{1,0:T(8,128)(2,1)S(1)} %collective-permute-done.4.even_ref, ...), custom_call_target="tpu_custom_call" | custom-call | flops 18874368 | bytes 294912 | tf_op jit(solution)/shard_map/join/pallas_call | solution.py:508
  (1 shorter events, 0.0 us)
Async XLA Ops:
  0.0 6.9 %collective-permute-start = (s32[1,3]{1,0:T(1,128)}, s32[1,3]{1,0:T(1,128)S(1)}, u32[]{:S(2)}, u32[]{:S(2)}) collective-permute-start(s32[1,3]{1,0:T(1,128)} %kind_hbm.1), channel_id=1, source_target_pairs={{0,2},{1,3},{2,0},{3,1},{4,6},{5,7},{6,4},{7,5},{8,10},{9,11},{10,... | collective-permute-start | bytes 44 | tf_op jit(solution)/shard_map/ppermute | solution.py:404
  4.2 2.7 %slice-start = ((s8[4718592]{0:T(1024)(128)(4,1)}), s8[4194304]{0:T(1024)(128)(4,1)S(1)}, s32[]{:S(2)}) async-start(s8[4718592]{0:T(1024)(128)(4,1)} %bitcast.1), calls=%async_computation | async-start | bytes 8388608
  4.2 2.7 %copy-start = (bf16[1,768,512]{2,1,0:T(8,128)(2,1)S(1)}, bf16[1,768,512]{2,1,0:T(8,128)(2,1)}, u32[]{:S(2)}) copy-start(bf16[1,768,512]{2,1,0:T(8,128)(2,1)} %x_ref.3) | copy-start | bytes 2359300
  4.2 2.7 %slice-start.1 = ((s8[4718592]{0:T(1024)(128)(4,1)}), s8[524288]{0:T(1024)(128)(4,1)S(1)}, s32[]{:S(2)}) async-start(s8[4718592]{0:T(1024)(128)(4,1)} %bitcast.1), calls=%async_computation.1 | async-start | bytes 1048576
  4.9 7.5 %collective-permute-start.3 = (bf16[80,288]{1,0:T(8,128)(2,1)S(1)}, bf16[80,288]{1,0:T(8,128)(2,1)S(1)}, u32[]{:S(2)}, u32[]{:S(2)}) collective-permute-start(bf16[80,288]{1,0:T(8,128)(2,1)S(1)} %get-tuple-element.46.rest_0_), channel_id=1, source_target_pairs={{0,24},{8,16},{16,8},{24,0},{1,25},{9,17},{17,9},{25,1},{2,26},{10... | collective-permute-start | bytes 138248 | tf_op jit(solution)/shard_map/ppermute | solution.py:404
  5.7 6.8 %collective-permute-start.2 = (bf16[80,288]{1,0:T(8,128)(2,1)S(1)}, bf16[80,288]{1,0:T(8,128)(2,1)S(1)}, u32[]{:S(2)}, u32[]{:S(2)}) collective-permute-start(bf16[80,288]{1,0:T(8,128)(2,1)S(1)} %get-tuple-element.46.rest_0_), channel_id=1, source_target_pairs={{0,16},{8,24},{16,0},{24,8},{1,17},{9,25},{17,1},{25,9},{2,18},{10... | collective-permute-start | bytes 138248 | tf_op jit(solution)/shard_map/ppermute | solution.py:404
  6.6 5.8 %collective-permute-start.1 = (bf16[80,288]{1,0:T(8,128)(2,1)S(1)}, bf16[80,288]{1,0:T(8,128)(2,1)S(1)}, u32[]{:S(2)}, u32[]{:S(2)}) collective-permute-start(bf16[80,288]{1,0:T(8,128)(2,1)S(1)} %get-tuple-element.46.rest_0_), channel_id=1, source_target_pairs={{0,8},{8,0},{16,24},{24,16},{1,9},{9,1},{17,25},{25,17},{2,10},{10... | collective-permute-start | bytes 138248 | tf_op jit(solution)/shard_map/ppermute | solution.py:404
  11.1 3.6 %collective-permute-start.5 = (bf16[80,128]{1,0:T(8,128)(2,1)S(1)}, bf16[80,128]{1,0:T(8,128)(2,1)S(1)}, u32[]{:S(2)}, u32[]{:S(2)}) collective-permute-start(bf16[80,128]{1,0:T(8,128)(2,1)S(1)} %get-tuple-element.43.own_ref), channel_id=1, source_target_pairs={{0,8},{7,15},{1,2},{2,1},{3,4},{4,3},{5,6},{6,5},{8,0},{15,7},{9,1... | collective-permute-start | bytes 61448 | tf_op jit(solution)/shard_map/ppermute | solution.py:414
  11.4 3.8 %collective-permute-start.4 = (bf16[80,128]{1,0:T(8,128)(2,1)S(1)}, bf16[80,128]{1,0:T(8,128)(2,1)S(1)}, u32[]{:S(2)}, u32[]{:S(2)}) collective-permute-start(bf16[80,128]{1,0:T(8,128)(2,1)S(1)} %get-tuple-element.43.own_ref), channel_id=1, source_target_pairs={{0,1},{1,0},{2,3},{3,2},{4,5},{5,4},{6,7},{7,6},{8,9},{9,8},{10,11... | collective-permute-start | bytes 61448 | tf_op jit(solution)/shard_map/ppermute | solution.py:404
where the time goes:
time: 16.3 us; the launch traced here: 16.2 us
  Pallas kernels  9.21 us (57%)
  starting transfers between devices  6.34 us (39%)
  waiting for transfers between devices  0.5 us (3%)
    ppermute x5, starting transfers between devices, exchange(): return lax.ppermute(value, axis, [(i, i ^ offset) for i in range(count)])  6.02 us
    pallas_call x1, Pallas kernels, local(): pl.pallas_call(functools.partial(middle_kernel, offsets), out_shape=[jax....  4.15 us
    pallas_call x1, Pallas kernels, local(): pl.pallas_call(functools.partial(final_kernel, dp), out_shape=[pltpu.VMEM...  2.19 us
    pallas_call x1, Pallas kernels, load(): pl.pallas_call(load_kernel, out_shape=[pltpu.SMEM((8,), jnp.int32), pltpu...  1.18 us
    pallas_call x1, Pallas kernels, local(): pl.pallas_call(join_kernel, out_shape=jax.ShapeDtypeStruct((1, 2 * tokens...  0.99 us
    pallas_call x1, Pallas kernels, local(): pl.pallas_call(begin_kernel, out_shape=[z_buffer, u_buffer, pltpu.VMEM((c...  0.69 us
    ppermute x5, waiting for transfers between devices, exchange(): return lax.ppermute(value, axis, [(i, i ^ offset) for i in range(count)])  0.5 us
  transfers between devices with their start and end apart: 6, of which 1 were waited for; matrix products, arithmetic and copies ran while one was open for 0% of the time, Pallas kernels for 51%

commit v1 on v0

--- a/solution.py
+++ b/solution.py
@@ -14,7 +14,6 @@
 LATENT_SCALE = 1.5305
 NORM_EPSILON = 1e-06
 LANES = 128
-ROW_STEPS = (0, -1, 1)
 VMEM_BYTES = 64 * 1024 * 1024
 F32 = jnp.float32
 BF16 = jnp.bfloat16
@@ -49,7 +48,11 @@
     return total, jnp.sum(half * half, axis=0, keepdims=True)
 
 
-def norm_first_steps(x_ref, joined, gain, shift, same_group, z_ref, u_ref):
+def halves_together(upper, lower):
+    return jnp.stack([upper, lower], axis=1)
+
+
+def norm_first_steps(x_ref, joined, gain, shift, same_group, v_ref):
     cells, channels = x_ref.shape
     half = cells // 2
     rows = cells // SLOT_COLS
@@ -65,7 +68,8 @@
         parts.append(jnp.concatenate([t0, t1, q0, q1], axis=0))
         yield
     scale, offset = affine(jnp.concatenate(parts, axis=1), joined, gain, shift, same_group, count)
-    zero = jnp.zeros((SLOT_COLS, LANES), F32)
+    zero = jnp.zeros((1, SLOT_COLS, LANES), F32)
+    mid = rows // 2
     for k in range(chunks):
         lanes = slice(k * LANES, (k + 1) * LANES)
         x = x_ref[:, lanes].astype(F32)
@@ -73,33 +77,32 @@
                              x[half:] * scale[1:2, lanes] + offset[1:2, lanes]], axis=0)
         act = v + v * jnp.tanh(v)
         act3 = act.reshape(rows, SLOT_COLS, LANES)
-        left = jnp.where(column == 0, 0.0, pltpu.roll(act3, 1, 1)).reshape(cells, LANES)
-        right = jnp.where(column == SLOT_COLS - 1, 0.0, pltpu.roll(act3, SLOT_COLS - 1, 1)).reshape(cells, LANES)
-        for b, value in enumerate((left, act, right)):
-            z_ref[b, :, lanes] = value.astype(BF16)
-            over = value[half:half + SLOT_COLS] * keep
-            under = value[half - SLOT_COLS:half] * keep
-            u_ref[b, 0, :, lanes] = jnp.concatenate([zero, value[:half], over], axis=0).astype(BF16)
-            u_ref[b, 1, :, lanes] = jnp.concatenate([under, value[half:], zero], axis=0).astype(BF16)
+        left = jnp.where(column == 0, 0.0, pltpu.roll(act3, 1, 1))
+        right = jnp.where(column == SLOT_COLS - 1, 0.0, pltpu.roll(act3, SLOT_COLS - 1, 1))
+        for b, value in enumerate((left, act3, right)):
+            upper, lower = value[:mid], value[mid:]
+            top = halves_together(zero, upper[mid - 1:] * keep)
+            bottom = halves_together(lower[:1] * keep, zero)
+            tiles = jnp.concatenate([top, halves_together(upper, lower), bottom], axis=0)
+            v_ref[b, :, lanes] = tiles.reshape(cells + 4 * SLOT_COLS, LANES).astype(BF16)
         yield
 
 
-def conv_steps(x_ref, bias, wbuf, wait_weights, z_ref, u_ref, y_ref):
+def conv_steps(x_ref, bias, w_ref, v_ref, y_ref):
     cells, channels = x_ref.shape
     half = cells // 2
     tile = channels // 2
-    totals = [x_ref[:, k * tile:(k + 1) * tile].astype(F32) + bias[:, k * tile:(k + 1) * tile] for k in range(2)]
-    for step, a in enumerate(ROW_STEPS):
-        wait_weights(step)
+    totals = []
+    for k in range(2):
+        lanes = slice(k * tile, (k + 1) * tile)
+        x = x_ref[:, lanes].astype(F32).reshape(2, half // SLOT_COLS, SLOT_COLS, tile)
+        totals.append(halves_together(x[0], x[1]).reshape(cells, tile) + bias[:, lanes])
+    for a in range(3):
         for b in range(3):
-            if a == 0:
-                lhs = z_ref[b]
-            else:
-                first = 0 if a < 0 else 2 * SLOT_COLS
-                lhs = jnp.concatenate([u_ref[b, h, first:first + half, :] for h in range(2)], axis=0)
-            base = (3 * (a + 1) + b) * channels
+            lhs = v_ref[b, 2 * SLOT_COLS * a:2 * SLOT_COLS * a + cells, :]
+            base = (3 * a + b) * channels
             for k in range(2):
-                totals[k] = totals[k] + jnp.dot(lhs, wbuf[base:base + channels, k * tile:(k + 1) * tile],
+                totals[k] = totals[k] + jnp.dot(lhs, w_ref[base:base + channels, k * tile:(k + 1) * tile],
                                                 preferred_element_type=F32)
                 yield
     for k in range(2):
@@ -123,23 +126,25 @@
 def norm_second_steps(y_ref, joined, gain, shift, same_group):
     cells, channels = y_ref.shape
     half = cells // 2
+    rows = half // SLOT_COLS
     chunks = channels // LANES
     count = half * (channels // GROUPS)
     parts = []
     for k in range(chunks):
-        lanes = slice(k * LANES, (k + 1) * LANES)
-        inner = y_ref[:, lanes].astype(F32)
-        t0, q0 = half_stats(inner[:half])
-        t1, q1 = half_stats(inner[half:])
+        inner = y_ref[:, k * LANES:(k + 1) * LANES].astype(F32).reshape(rows, 2, SLOT_COLS, LANES)
+        t0, q0 = half_stats(inner[:, 0].reshape(half, LANES))
+        t1, q1 = half_stats(inner[:, 1].reshape(half, LANES))
         parts.append(jnp.concatenate([t0, t1, q0, q1], axis=0))
         yield
     scale, offset = affine(jnp.concatenate(parts, axis=1), joined, gain, shift, same_group, count)
     for k in range(chunks):
         lanes = slice(k * LANES, (k + 1) * LANES)
-        y = y_ref[:, lanes].astype(F32)
-        v = jnp.concatenate([y[:half] * scale[0:1, lanes] + offset[0:1, lanes],
-                             y[half:] * scale[1:2, lanes] + offset[1:2, lanes]], axis=0)
-        y_ref[:, lanes] = (v + v * jnp.tanh(v)).astype(BF16)
+        y = y_ref[:, lanes].astype(F32).reshape(rows, 2, SLOT_COLS, LANES)
+        acts = []
+        for h in range(2):
+            v = y[:, h].reshape(half, LANES) * scale[h:h + 1, lanes] + offset[h:h + 1, lanes]
+            acts.append((v + v * jnp.tanh(v)).reshape(rows, SLOT_COLS, LANES))
+        y_ref[:, lanes] = halves_together(*acts).reshape(cells, LANES).astype(BF16)
         yield
 
 
@@ -158,9 +163,11 @@
     moved = here + jnp.where(column == 0, 0.0, pltpu.roll(from_left, 1, 1))
     moved = moved + jnp.where(column == SLOT_COLS - 1, 0.0, pltpu.roll(from_right, SLOT_COLS - 1, 1))
     yield
+    moved = moved.reshape(mid, 2, SLOT_COLS, LANES)
+    upper, lower = moved[:, 0], moved[:, 1]
     blank = jnp.zeros((1, SLOT_COLS, LANES), F32)
-    above = jnp.concatenate([blank, moved[:mid - 1], moved[mid - 1:mid] * keep, moved[mid:rows - 1]], axis=0)
-    below = jnp.concatenate([moved[1:mid], moved[mid:mid + 1] * keep, moved[mid + 1:], blank], axis=0)
+    above = jnp.concatenate([halves_together(blank, upper[mid - 1:] * keep), moved[:mid - 1]], axis=0)
+    below = jnp.concatenate([moved[1:], halves_together(lower[:1] * keep, blank)], axis=0)
     step_up = (block == 0) | (block == 3)
     step_none = (block == 1) | (block == 4)
     mixed = jnp.where(step_up, above, jnp.where(step_none, moved, below)).reshape(cells, LANES)
@@ -168,8 +175,8 @@
     latent = mixed + pltpu.roll(mixed, LANES - lat, 1) + pltpu.roll(mixed, LANES - 2 * lat, 1)
     latent = ((latent + bias) - LATENT_SHIFT) * LATENT_SCALE
     corner = block - part(lax.broadcasted_iota(jnp.int32, (1, SLOT_COLS, LANES), 1), 2)
-    corner = jnp.concatenate([corner, corner - 2], axis=0)
-    latent = latent.reshape(rows // 2, 2, SLOT_COLS, LANES)
+    corner = jnp.stack([corner, corner - 2], axis=0)
+    latent = latent.reshape(mid // 2, 2, 2, SLOT_COLS, LANES)
     latent = jnp.where((corner == 0)[None], latent, 0.0).reshape(cells, LANES)
     yield
     store(jnp.dot(gather, latent.astype(BF16), preferred_element_type=F32)[:, :4 * lat].astype(BF16))
@@ -206,7 +213,8 @@
     half_cols = SLOT_COLS // 2
     token = lax.broadcasted_iota(jnp.int32, (cells // 4, cells), 0)
     cell = lax.broadcasted_iota(jnp.int32, (cells // 4, cells), 1)
-    own = whole(whole(cell, SLOT_COLS), 2) * half_cols + whole(part(cell, SLOT_COLS), 2)
+    row_pair = whole(cell, 4 * SLOT_COLS) + part(whole(cell, SLOT_COLS), 2) * (cells // (4 * SLOT_COLS))
+    own = row_pair * half_cols + whole(part(cell, SLOT_COLS), 2)
     return jnp.where(own == token, 1.0, 0.0).astype(BF16)
 
 
@@ -253,11 +261,11 @@
 
 
 def begin_kernel(state_ref, x_ref, gain_ref, shift_ref, lw_ref, lb_ref, piece_in,
-                 z_ref, u_ref, table_ref, bias4_ref, perm_ref, piece_ref):
+                 v_ref, table_ref, bias4_ref, perm_ref, piece_ref):
     piece_ref[...] = piece_in[...]
     perm_ref[...] = patch_table(x_ref.shape[0])
     interleave(norm_first_steps(x_ref, state_ref[2 + FIRST] == 2, vector(gain_ref), vector(shift_ref),
-                                group_table(x_ref.shape[1]), z_ref, u_ref),
+                                group_table(x_ref.shape[1]), v_ref),
                patch_tables(lw_ref, lb_ref, table_ref, bias4_ref))
 
 
@@ -281,12 +289,12 @@
     return total
 
 
-def middle_kernel(offsets, state_ref, x_ref, w_ref, perm_ref, z_ref, u_ref, *rest):
+def middle_kernel(offsets, state_ref, x_ref, w_ref, perm_ref, v_ref, *rest):
     names = 7
     small, rest = rest[:names], rest[names:]
     others, rest = rest[:len(offsets)], rest[len(offsets):]
-    message_ref, sums_ref, z3_ref, u3_ref, *rest = rest
-    early_ref, y_ref, z2_ref, u2_ref, *rest = rest
+    message_ref, sums_ref, v3_ref, *rest = rest
+    early_ref, y_ref, v2_ref, *rest = rest
     kinds, ksem = rest[:-1], rest[-1]
     copies = [pltpu.make_async_copy(src, dst, ksem.at[i]) for i, (src, dst) in enumerate(zip(others, kinds))]
     for c in copies:
@@ -299,9 +307,9 @@
     def features_of(at):
         return x_ref.at[0, pl.ds(pl.multiple_of(at * cells, cells), cells), :]
 
-    def first_norm(at, z_to, u_to):
+    def first_norm(at, to_ref):
         return norm_first_steps(features_of(at), state_ref[2 + at] == 2, vector(small[0]), vector(small[1]),
-                                group_table(x_ref.shape[2]), z_to, u_to)
+                                group_table(x_ref.shape[2]), to_ref)
 
     def encode_two(with_third):
         found = {}
@@ -312,10 +320,10 @@
             return store
 
         kind, early_kind = state_ref[2 + slot], state_ref[2 + FIRST]
-        third = [first_norm(0, z3_ref, u3_ref)] if with_third else []
-        interleave(conv_steps(features_of(FIRST), vector(small[2]), w_ref, lambda step: None, z_ref, u_ref, early_ref),
-                   first_norm(slot, z2_ref, u2_ref))
-        interleave(conv_steps(features_of(slot), vector(small[2]), w_ref, lambda step: None, z2_ref, u2_ref, y_ref),
+        third = [first_norm(0, v3_ref)] if with_third else []
+        interleave(conv_steps(features_of(FIRST), vector(small[2]), w_ref, v_ref, early_ref),
+                   first_norm(slot, v2_ref))
+        interleave(conv_steps(features_of(slot), vector(small[2]), w_ref, v2_ref, y_ref),
                    chain(second_norm(early_ref, early_kind, small), *third))
         interleave(chain(second_norm(y_ref, kind, small), patches(keep_as("second"), y_ref, kind, small, perm_ref)),
                    patches(keep_as("first"), early_ref, early_kind, small, perm_ref))
@@ -343,7 +351,7 @@
     message_ref[tokens:, :] = jnp.full((message_ref.shape[0] - tokens, 2 * feats), told.astype(F32)).astype(BF16)
 
 
-def final_kernel(parts, state_ref, x_ref, w_ref, perm_ref, z_ref, u_ref, *rest):
+def final_kernel(parts, state_ref, x_ref, w_ref, perm_ref, v_ref, *rest):
     pieces, small, rest = rest[:parts], rest[parts:parts + 7], rest[parts + 7:]
     out_ref, embed_ref, y_ref = rest
     group = lax.axis_index("dp")
@@ -362,7 +370,7 @@
         def store(value):
             out_ref[...] = value
 
-        interleave(conv_steps(x_ref.at[0, 0:y_ref.shape[0], :], vector(small[2]), w_ref, lambda step: None, z_ref, u_ref, y_ref),
+        interleave(conv_steps(x_ref.at[0, 0:y_ref.shape[0], :], vector(small[2]), w_ref, v_ref, y_ref),
                    lay_out())
         drain(second_norm(y_ref, state_ref[2], small))
         drain(patches(store, y_ref, state_ref[2], small, perm_ref))
@@ -468,43 +476,42 @@
     slot_buffer = pltpu.VMEM((cells, channels), BF16)
     flops = encode_flops(cells, channels, latent_bias.shape[0])
     state, x, piece, *small = load(features, slot_kind, embed_weight, embed_bias, small)
-    z_buffer = pltpu.VMEM((3, cells, channels), BF16)
-    u_buffer = pltpu.VMEM((3, 2, cells // 2 + 2 * SLOT_COLS, channels), BF16)
-    z, u, table, bias4, perm, piece = pl.pallas_call(
+    v_buffer = pltpu.VMEM((3, cells + 4 * SLOT_COLS, channels), BF16)
+    v, table, bias4, perm, piece = pl.pallas_call(
         begin_kernel,
-        out_shape=[z_buffer, u_buffer, pltpu.VMEM((channels, 3 * LANES), BF16), pltpu.VMEM((1, LANES), F32),
+        out_shape=[v_buffer, pltpu.VMEM((channels, 3 * LANES), BF16), pltpu.VMEM((1, LANES), F32),
                    pltpu.VMEM((tokens, cells), BF16), pltpu.VMEM(piece.shape, BF16)],
         in_specs=[SMEM_SPEC] + [VMEM_SPEC] * 6,
-        out_specs=[VMEM_SPEC] * 6,
+        out_specs=[VMEM_SPEC] * 5,
         compiler_params=pltpu.CompilerParams(vmem_limit_bytes=16 * MIB),
         cost_estimate=cost(2 * flops, features.size),
         name="begin",
     )(state, x, *small[:2], *small[5:], piece)
     small = (*small[:5], table, bias4)
-    message, sums, z3, u3 = pl.pallas_call(
+    message, sums, v3 = pl.pallas_call(
         functools.partial(middle_kernel, offsets),
-        out_shape=[jax.ShapeDtypeStruct((tokens + 16, 2 * feats), BF16), pltpu.SMEM((1,), jnp.int32), z_buffer, u_buffer],
-        in_specs=[SMEM_SPEC] + [VMEM_SPEC] * (5 + len(small)) + [ANY_SPEC] * len(others),
-        out_specs=[VMEM_SPEC, SMEM_SPEC] + [VMEM_SPEC] * 2,
-        scratch_shapes=[slot_buffer] * 2 + [z_buffer, u_buffer] + [pltpu.SMEM(slot_kind.shape, jnp.int32) for _ in others]
+        out_shape=[jax.ShapeDtypeStruct((tokens + 16, 2 * feats), BF16), pltpu.SMEM((1,), jnp.int32), v_buffer],
+        in_specs=[SMEM_SPEC] + [VMEM_SPEC] * (4 + len(small)) + [ANY_SPEC] * len(others),
+        out_specs=[VMEM_SPEC, SMEM_SPEC, VMEM_SPEC],
+        scratch_shapes=[slot_buffer] * 2 + [v_buffer] + [pltpu.SMEM(slot_kind.shape, jnp.int32) for _ in others]
         + [pltpu.SemaphoreType.DMA((len(others),))],
         compiler_params=pltpu.CompilerParams(vmem_limit_bytes=16 * MIB),
         cost_estimate=cost(flops, block_weight.size * 2),
         name="middle",
-    )(state, features, block_weight, perm, z, u, *small, *others)
+    )(state, features, block_weight, perm, v, *small, *others)
     even = exchange(message, "seq", 1)
     odd = swap_odd_pairs(message)
     pieces = [piece] + [exchange(piece, "dp", offset) for offset in range(1, dp)]
     third, embed = pl.pallas_call(
         functools.partial(final_kernel, dp),
         out_shape=[pltpu.VMEM((tokens, feats), BF16), pltpu.VMEM((feats + 16, dp * width), BF16)],
-        in_specs=[SMEM_SPEC] + [VMEM_SPEC] * (5 + dp + len(small)),
+        in_specs=[SMEM_SPEC] + [VMEM_SPEC] * (4 + dp + len(small)),
         out_specs=[VMEM_SPEC] * 2,
         scratch_shapes=[slot_buffer],
         compiler_params=pltpu.CompilerParams(vmem_limit_bytes=16 * MIB),
         cost_estimate=cost(flops, block_weight.size * 2),
         name="final",
-    )(state, features, block_weight, perm, z3, u3, *pieces, *small)
+    )(state, features, block_weight, perm, v3, *pieces, *small)
     return pl.pallas_call(
         join_kernel,
         out_shape=jax.ShapeDtypeStruct((1, 2 * tokens, dp * width), BF16),

time: 16.3 us -> 15.9 us (0.975)
  Pallas kernels: 9.21 us -> 8.93 us
    pallas_call x1, Pallas kernels: 4.15 us -> 3.97 us  [local(): pl.pallas_call(functools.partial(middle_kernel, offsets), out_shape=[jax....]
  transfers between devices with their start and end apart: 6 -> 6, of which waited for: 1 -> 1; matrix products, arithmetic and copies ran while one was open for 0% -> 0% of each run, Pallas kernels for 51% -> 50%
where the time goes in v1:
time: 15.9 us
  Pallas kernels  8.93 us (56%)
  starting transfers between devices  6.39 us (40%)
  waiting for transfers between devices  0.44 us (3%)
    ppermute x5, starting transfers between devices, exchange(): return lax.ppermute(value, axis, [(i, i ^ offset) for i in range(count)])  6.08 us
    pallas_call x1, Pallas kernels, local(): pl.pallas_call(functools.partial(middle_kernel, offsets), out_shape=[jax....  3.97 us
    pallas_call x1, Pallas kernels, local(): pl.pallas_call(functools.partial(final_kernel, dp), out_shape=[pltpu.VMEM...  2.2 us
    pallas_call x1, Pallas kernels, load(): pl.pallas_call(load_kernel, out_shape=[pltpu.SMEM((8,), jnp.int32), pltpu...  1.18 us
    pallas_call x1, Pallas kernels, local(): pl.pallas_call(join_kernel, out_shape=jax.ShapeDtypeStruct((1, 2 * tokens...  0.99 us
    pallas_call x1, Pallas kernels, local(): pl.pallas_call(begin_kernel, out_shape=[v_buffer, pltpu.VMEM((channels, 3...  0.58 us
    ppermute x5, waiting for transfers between devices, exchange(): return lax.ppermute(value, axis, [(i, i ^ offset) for i in range(count)])  0.43 us
  transfers between devices with their start and end apart: 6, of which 1 were waited for; matrix products, arithmetic and copies ran while one was open for 0% of the time, Pallas kernels for 50%

profile of v1, /device:TPU:0, one launch (start us, length us, event | category | flops | bytes accessed | tf_op | source)
XLA Modules:
  0.0 15.9 jit_solution(5064836720277319257)
XLA Ops:
  0.0 3.0 %collective-permute-start = (s32[1,3]{1,0:T(1,128)}, s32[1,3]{1,0:T(1,128)S(1)}, u32[]{:S(2)}, u32[]{:S(2)}) collective-permute-start(s32[1,3]{1,0:T(1,128)} %kind_hbm.1), channel_id=1, source_target_pairs={{0,2},{1,3},{2,0},{3,1},{4,6},{5,7},{6,4},{7,5},{8,10},{9,11},{10,... | collective-permute-start | bytes 44 | tf_op jit(solution)/shard_map/ppermute | solution.py:412
  3.0 1.2 %load.1 = (s32[8]{0:T(128)S(4)}, bf16[256,512]{1,0:T(8,128)(2,1)S(1)}, bf16[80,288]{1,0:T(8,128)(2,1)S(1)}, f32[512]{0:T(512)S(1)}, f32[512]{0:T(512)S(1)}, /*in...) custom-call(s32[1,3]{1,0:T(1,128)} %kind_hbm.1, ...), custom_call_target="tpu_custom_call" | custom-call | bytes 393216 | tf_op jit(solution)/shard_map/load/pallas_call | solution.py:443
  4.2 0.0 slice-start
  4.2 0.0 copy-start
  4.2 0.0 slice-start.1
  4.2 0.6 %begin.1 = (bf16[3,288,512]{2,1,0:T(8,128)(2,1)S(1)}, bf16[512,384]{1,0:T(8,128)(2,1)S(1)}, f32[1,128]{1,0:T(1,128)S(1)}, bf16[64,256]{1,0:T(8,128)(2,1)S(1)}, bf16[80,288]{1,0:T(8,128)(2,1)S(1)}) custom-call(s32[8]{0:T(128)S(4)} %get-tuple-element.25.state_ref, bf16[256,512]{1,0:T(8,128)(2,1)S(1)} %get-tuple-element.26.x_ref, ...), custom_call_target="tpu_custom_call" | custom-call | flops 2491416576 | bytes 393216 | tf_op jit(solution)/shard_map/begin/pallas_call | solution.py:480
  4.8 0.7 %collective-permute-start.3 = (bf16[80,288]{1,0:T(8,128)(2,1)S(1)}, bf16[80,288]{1,0:T(8,128)(2,1)S(1)}, u32[]{:S(2)}, u32[]{:S(2)}) collective-permute-start(bf16[80,288]{1,0:T(8,128)(2,1)S(1)} %get-tuple-element.42.rest_0_), channel_id=1, source_target_pairs={{0,24},{8,16},{16,8},{24,0},{1,25},{9,17},{17,9},{25,1},{2,26},{10... | collective-permute-start | bytes 138248 | tf_op jit(solution)/shard_map/ppermute | solution.py:412
  5.6 0.9 %collective-permute-start.2 = (bf16[80,288]{1,0:T(8,128)(2,1)S(1)}, bf16[80,288]{1,0:T(8,128)(2,1)S(1)}, u32[]{:S(2)}, u32[]{:S(2)}) collective-permute-start(bf16[80,288]{1,0:T(8,128)(2,1)S(1)} %get-tuple-element.42.rest_0_), channel_id=1, source_target_pairs={{0,16},{8,24},{16,0},{24,8},{1,17},{9,25},{17,1},{25,9},{2,18},{10... | collective-permute-start | bytes 138248 | tf_op jit(solution)/shard_map/ppermute | solution.py:412
  6.5 0.3 %collective-permute-start.1 = (bf16[80,288]{1,0:T(8,128)(2,1)S(1)}, bf16[80,288]{1,0:T(8,128)(2,1)S(1)}, u32[]{:S(2)}, u32[]{:S(2)}) collective-permute-start(bf16[80,288]{1,0:T(8,128)(2,1)S(1)} %get-tuple-element.42.rest_0_), channel_id=1, source_target_pairs={{0,8},{8,0},{16,24},{24,16},{1,9},{9,1},{17,25},{25,17},{2,10},{10... | collective-permute-start | bytes 138248 | tf_op jit(solution)/shard_map/ppermute | solution.py:412
  6.8 0.0 collective-permute-done.rest_7_
  6.8 0.0 slice-done
  6.8 0.0 copy-done
  6.8 0.0 slice-done.1
  6.8 4.0 %middle.1 = (bf16[80,128]{1,0:T(8,128)(2,1)S(1)}, s32[1]{0:T(128)S(4)}, bf16[3,288,512]{2,1,0:T(8,128)(2,1)S(1)}) custom-call(s32[8]{0:T(128)S(4)} %get-tuple-element.25.state_ref, bf16[1,768,512]{2,1,0:T(8,128)(2,1)S(1)} %copy-done, bf16[4608,512]{1,0:T(8,128)(2,1)S(1)} %bitcast.2, bf16[64,256]{1,0:T(8,128)(2,1)S(1)} %get-tuple-element.32.perm_ref, ...), custom_call_target="tpu_custom_call" | custom-call | flops 1245708288 | bytes 4718592 | tf_op jit(solution)/shard_map/middle/pallas_call | solution.py:491
  10.8 0.3 %collective-permute-start.5 = (bf16[80,128]{1,0:T(8,128)(2,1)S(1)}, bf16[80,128]{1,0:T(8,128)(2,1)S(1)}, u32[]{:S(2)}, u32[]{:S(2)}) collective-permute-start(bf16[80,128]{1,0:T(8,128)(2,1)S(1)} %get-tuple-element.40.own_ref), channel_id=1, source_target_pairs={{0,8},{7,15},{1,2},{2,1},{3,4},{4,3},{5,6},{6,5},{8,0},{15,7},{9,1... | collective-permute-start | bytes 61448 | tf_op jit(solution)/shard_map/ppermute | solution.py:422
  11.1 1.1 %collective-permute-start.4 = (bf16[80,128]{1,0:T(8,128)(2,1)S(1)}, bf16[80,128]{1,0:T(8,128)(2,1)S(1)}, u32[]{:S(2)}, u32[]{:S(2)}) collective-permute-start(bf16[80,128]{1,0:T(8,128)(2,1)S(1)} %get-tuple-element.40.own_ref), channel_id=1, source_target_pairs={{0,1},{1,0},{2,3},{3,2},{4,5},{5,4},{6,7},{7,6},{8,9},{9,8},{10,11... | collective-permute-start | bytes 61448 | tf_op jit(solution)/shard_map/ppermute | solution.py:412
  12.2 0.0 collective-permute-done.3.rest_3_
  12.2 0.0 collective-permute-done.2.rest_2_
  12.2 0.0 collective-permute-done.1.rest_1_
  12.2 2.2 %final.1 = (bf16[64,64]{1,0:T(8,128)(2,1)S(1)}, bf16[80,1152]{1,0:T(8,128)(2,1)S(1)}) custom-call(s32[8]{0:T(128)S(4)} %get-tuple-element.25.state_ref, bf16[1,768,512]{2,1,0:T(8,128)(2,1)S(1)} %copy-done, bf16[4608,512]{1,0:T(8,128)(2,1)S(1)} %bitcast.2, bf16[64,256]{1,0:T(8,128)(2,1)S(1)} %get-tuple-element.32.perm_ref, ...), custom_call_target="tpu_custom_call" | custom-call | flops 1245708288 | bytes 4718592 | tf_op jit(solution)/shard_map/final/pallas_call | solution.py:505
  14.4 0.0 collective-permute-done.5.odd_ref
  14.4 0.4 %collective-permute-done.4.even_ref = bf16[80,128]{1,0:T(8,128)(2,1)S(1)} collective-permute-done((bf16[80,128]{1,0:T(8,128)(2,1)S(1)}, bf16[80,128]{1,0:T(8,128)(2,1)S(1)}, u32[]{:S(2)}, u32[]{:S(2)}) %collective-permute-start.4) | collective-permute-done | bytes 20512 | tf_op jit(solution)/shard_map/ppermute | solution.py:412
  14.9 1.0 %join.1 = bf16[1,128,1152]{2,1,0:T(8,128)(2,1)} custom-call(s32[8]{0:T(128)S(4)} %get-tuple-element.25.state_ref, s32[1]{0:T(128)S(4)} %get-tuple-element.39.sums_ref, bf16[80,128]{1,0:T(8,128)(2,1)S(1)} %get-tuple-element.40.own_ref, bf16[64,64]{1,0:T(8,128)(2,1)S(1)} %get-tuple-element.43.third_ref, bf16[80,128]{1,0:T(8,128)(2,1)S(1)} %collective-permute-done.4.even_ref, ...), custom_call_target="tpu_custom_call" | custom-call | flops 18874368 | bytes 294912 | tf_op jit(solution)/shard_map/join/pallas_call | solution.py:515
  (1 shorter events, 0.0 us)
Async XLA Ops:
  0.0 6.8 %collective-permute-start = (s32[1,3]{1,0:T(1,128)}, s32[1,3]{1,0:T(1,128)S(1)}, u32[]{:S(2)}, u32[]{:S(2)}) collective-permute-start(s32[1,3]{1,0:T(1,128)} %kind_hbm.1), channel_id=1, source_target_pairs={{0,2},{1,3},{2,0},{3,1},{4,6},{5,7},{6,4},{7,5},{8,10},{9,11},{10,... | collective-permute-start | bytes 44 | tf_op jit(solution)/shard_map/ppermute | solution.py:412
  4.2 2.6 %slice-start = ((s8[4718592]{0:T(1024)(128)(4,1)}), s8[4194304]{0:T(1024)(128)(4,1)S(1)}, s32[]{:S(2)}) async-start(s8[4718592]{0:T(1024)(128)(4,1)} %bitcast.1), calls=%async_computation | async-start | bytes 8388608
  4.2 2.5 %copy-start = (bf16[1,768,512]{2,1,0:T(8,128)(2,1)S(1)}, bf16[1,768,512]{2,1,0:T(8,128)(2,1)}, u32[]{:S(2)}) copy-start(bf16[1,768,512]{2,1,0:T(8,128)(2,1)} %x_ref.3) | copy-start | bytes 2359300
  4.2 2.5 %slice-start.1 = ((s8[4718592]{0:T(1024)(128)(4,1)}), s8[524288]{0:T(1024)(128)(4,1)S(1)}, s32[]{:S(2)}) async-start(s8[4718592]{0:T(1024)(128)(4,1)} %bitcast.1), calls=%async_computation.1 | async-start | bytes 1048576
  4.8 7.4 %collective-permute-start.3 = (bf16[80,288]{1,0:T(8,128)(2,1)S(1)}, bf16[80,288]{1,0:T(8,128)(2,1)S(1)}, u32[]{:S(2)}, u32[]{:S(2)}) collective-permute-start(bf16[80,288]{1,0:T(8,128)(2,1)S(1)} %get-tuple-element.42.rest_0_), channel_id=1, source_target_pairs={{0,24},{8,16},{16,8},{24,0},{1,25},{9,17},{17,9},{25,1},{2,26},{10... | collective-permute-start | bytes 138248 | tf_op jit(solution)/shard_map/ppermute | solution.py:412
  5.6 6.6 %collective-permute-start.2 = (bf16[80,288]{1,0:T(8,128)(2,1)S(1)}, bf16[80,288]{1,0:T(8,128)(2,1)S(1)}, u32[]{:S(2)}, u32[]{:S(2)}) collective-permute-start(bf16[80,288]{1,0:T(8,128)(2,1)S(1)} %get-tuple-element.42.rest_0_), channel_id=1, source_target_pairs={{0,16},{8,24},{16,0},{24,8},{1,17},{9,25},{17,1},{25,9},{2,18},{10... | collective-permute-start | bytes 138248 | tf_op jit(solution)/shard_map/ppermute | solution.py:412
  6.5 5.7 %collective-permute-start.1 = (bf16[80,288]{1,0:T(8,128)(2,1)S(1)}, bf16[80,288]{1,0:T(8,128)(2,1)S(1)}, u32[]{:S(2)}, u32[]{:S(2)}) collective-permute-start(bf16[80,288]{1,0:T(8,128)(2,1)S(1)} %get-tuple-element.42.rest_0_), channel_id=1, source_target_pairs={{0,8},{8,0},{16,24},{24,16},{1,9},{9,1},{17,25},{25,17},{2,10},{10... | collective-permute-start | bytes 138248 | tf_op jit(solution)/shard_map/ppermute | solution.py:412
  10.8 3.7 %collective-permute-start.5 = (bf16[80,128]{1,0:T(8,128)(2,1)S(1)}, bf16[80,128]{1,0:T(8,128)(2,1)S(1)}, u32[]{:S(2)}, u32[]{:S(2)}) collective-permute-start(bf16[80,128]{1,0:T(8,128)(2,1)S(1)} %get-tuple-element.40.own_ref), channel_id=1, source_target_pairs={{0,8},{7,15},{1,2},{2,1},{3,4},{4,3},{5,6},{6,5},{8,0},{15,7},{9,1... | collective-permute-start | bytes 61448 | tf_op jit(solution)/shard_map/ppermute | solution.py:422
  11.1 3.8 %collective-permute-start.4 = (bf16[80,128]{1,0:T(8,128)(2,1)S(1)}, bf16[80,128]{1,0:T(8,128)(2,1)S(1)}, u32[]{:S(2)}, u32[]{:S(2)}) collective-permute-start(bf16[80,128]{1,0:T(8,128)(2,1)S(1)} %get-tuple-element.40.own_ref), channel_id=1, source_target_pairs={{0,1},{1,0},{2,3},{3,2},{4,5},{5,4},{6,7},{7,6},{8,9},{9,8},{10,11... | collective-permute-start | bytes 61448 | tf_op jit(solution)/shard_map/ppermute | solution.py:412

commit v2 on v1

--- a/solution.py
+++ b/solution.py
@@ -293,7 +293,7 @@
     names = 7
     small, rest = rest[:names], rest[names:]
     others, rest = rest[:len(offsets)], rest[len(offsets):]
-    message_ref, sums_ref, v3_ref, *rest = rest
+    message_ref, sums_ref, _, *rest = rest
     early_ref, y_ref, v2_ref, *rest = rest
     kinds, ksem = rest[:-1], rest[-1]
     copies = [pltpu.make_async_copy(src, dst, ksem.at[i]) for i, (src, dst) in enumerate(zip(others, kinds))]
@@ -311,29 +311,25 @@
         return norm_first_steps(features_of(at), state_ref[2 + at] == 2, vector(small[0]), vector(small[1]),
                                 group_table(x_ref.shape[2]), to_ref)
 
-    def encode_two(with_third):
-        found = {}
-
-        def keep_as(name):
-            def store(value):
-                found[name] = value
-            return store
-
-        kind, early_kind = state_ref[2 + slot], state_ref[2 + FIRST]
-        third = [first_norm(0, v3_ref)] if with_third else []
-        interleave(conv_steps(features_of(FIRST), vector(small[2]), w_ref, v_ref, early_ref),
-                   first_norm(slot, v2_ref))
-        interleave(conv_steps(features_of(slot), vector(small[2]), w_ref, v2_ref, y_ref),
-                   chain(second_norm(early_ref, early_kind, small), *third))
-        interleave(chain(second_norm(y_ref, kind, small), patches(keep_as("second"), y_ref, kind, small, perm_ref)),
-                   patches(keep_as("first"), early_ref, early_kind, small, perm_ref))
-        first_is_last = state_ref[0] == 2
-        last = jnp.where(first_is_last, found["first"], found["second"])
-        before = jnp.where(first_is_last, found["second"], found["first"])
-        message_ref[0:tokens, :] = jnp.concatenate([last, before], axis=1)
-
-    pl.when(state_ref[0] > 2)(lambda: encode_two(True))
-    pl.when(state_ref[0] <= 2)(lambda: encode_two(False))
+    found = {}
+
+    def keep_as(name):
+        def store(value):
+            found[name] = value
+        return store
+
+    kind, early_kind = state_ref[2 + slot], state_ref[2 + FIRST]
+    interleave(conv_steps(features_of(FIRST), vector(small[2]), w_ref, v_ref, early_ref),
+               first_norm(slot, v2_ref))
+    interleave(conv_steps(features_of(slot), vector(small[2]), w_ref, v2_ref, y_ref),
+               second_norm(early_ref, early_kind, small))
+    interleave(chain(second_norm(y_ref, kind, small), patches(keep_as("second"), y_ref, kind, small, perm_ref)),
+               patches(keep_as("first"), early_ref, early_kind, small, perm_ref))
+    first_is_last = state_ref[0] == 2
+    last = jnp.where(first_is_last, found["first"], found["second"])
+    before = jnp.where(first_is_last, found["second"], found["first"])
+    message_ref[0:tokens, :] = jnp.concatenate([last, before], axis=1)
+
     for c in copies:
         c.wait()
     position = lax.axis_index("seq")
@@ -351,9 +347,9 @@
     message_ref[tokens:, :] = jnp.full((message_ref.shape[0] - tokens, 2 * feats), told.astype(F32)).astype(BF16)
 
 
-def final_kernel(parts, state_ref, x_ref, w_ref, perm_ref, v_ref, *rest):
+def final_kernel(parts, state_ref, x_ref, w_ref, perm_ref, _, *rest):
     pieces, small, rest = rest[:parts], rest[parts:parts + 7], rest[parts + 7:]
-    out_ref, embed_ref, y_ref = rest
+    out_ref, embed_ref, y_ref, v_ref = rest
     group = lax.axis_index("dp")
     width = pieces[0].shape[1]
 
@@ -370,8 +366,10 @@
         def store(value):
             out_ref[...] = value
 
-        interleave(conv_steps(x_ref.at[0, 0:y_ref.shape[0], :], vector(small[2]), w_ref, v_ref, y_ref),
-                   lay_out())
+        x = x_ref.at[0, 0:y_ref.shape[0], :]
+        interleave(norm_first_steps(x, state_ref[2] == 2, vector(small[0]), vector(small[1]),
+                                    group_table(y_ref.shape[1]), v_ref), lay_out())
+        drain(conv_steps(x, vector(small[2]), w_ref, v_ref, y_ref))
         drain(second_norm(y_ref, state_ref[2], small))
         drain(patches(store, y_ref, state_ref[2], small, perm_ref))
 
@@ -488,7 +486,7 @@
         name="begin",
     )(state, x, *small[:2], *small[5:], piece)
     small = (*small[:5], table, bias4)
-    message, sums, v3 = pl.pallas_call(
+    message, sums, spare = pl.pallas_call(
         functools.partial(middle_kernel, offsets),
         out_shape=[jax.ShapeDtypeStruct((tokens + 16, 2 * feats), BF16), pltpu.SMEM((1,), jnp.int32), v_buffer],
         in_specs=[SMEM_SPEC] + [VMEM_SPEC] * (4 + len(small)) + [ANY_SPEC] * len(others),
@@ -507,11 +505,11 @@
         out_shape=[pltpu.VMEM((tokens, feats), BF16), pltpu.VMEM((feats + 16, dp * width), BF16)],
         in_specs=[SMEM_SPEC] + [VMEM_SPEC] * (4 + dp + len(small)),
         out_specs=[VMEM_SPEC] * 2,
-        scratch_shapes=[slot_buffer],
+        scratch_shapes=[slot_buffer, v_buffer],
         compiler_params=pltpu.CompilerParams(vmem_limit_bytes=16 * MIB),
         cost_estimate=cost(flops, block_weight.size * 2),
         name="final",
-    )(state, features, block_weight, perm, v3, *pieces, *small)
+    )(state, features, block_weight, perm, spare, *pieces, *small)
     return pl.pallas_call(
         join_kernel,
         out_shape=jax.ShapeDtypeStruct((1, 2 * tokens, dp * width), BF16),

time: 15.9 us -> 15.9 us (level)
  waiting for transfers between devices: 0.44 us -> 0.02 us
  starting transfers between devices: 6.39 us -> 6.71 us
    ppermute x5, waiting for transfers between devices: 0.43 us -> 0.01 us  [exchange(): return lax.ppermute(value, axis, [(i, i ^ offset) for i in range(count)])]
    pallas_call x1, Pallas kernels: 3.97 us -> 3.64 us  [local(): pl.pallas_call(functools.partial(middle_kernel, offsets), out_shape=[jax....]
    ppermute x5, starting transfers between devices: 6.08 us -> 6.4 us  [exchange(): return lax.ppermute(value, axis, [(i, i ^ offset) for i in range(count)])]
    pallas_call x1, Pallas kernels: 2.2 us -> 2.49 us  [local(): pl.pallas_call(functools.partial(final_kernel, dp), out_shape=[pltpu.VMEM...]
  transfers between devices with their start and end apart: 6 -> 6, of which waited for: 1 -> 0; matrix products, arithmetic and copies ran while one was open for 0% -> 0% of each run, Pallas kernels for 50% -> 50%
where the time goes in v2:
time: 15.9 us; the launch traced here: 15.7 us
  Pallas kernels  8.88 us (56%)
  starting transfers between devices  6.71 us (42%)
    ppermute x5, starting transfers between devices, exchange(): return lax.ppermute(value, axis, [(i, i ^ offset) for i in range(count)])  6.4 us
    pallas_call x1, Pallas kernels, local(): pl.pallas_call(functools.partial(middle_kernel, offsets), out_shape=[jax....  3.64 us
    pallas_call x1, Pallas kernels, local(): pl.pallas_call(functools.partial(final_kernel, dp), out_shape=[pltpu.VMEM...  2.49 us
    pallas_call x1, Pallas kernels, load(): pl.pallas_call(load_kernel, out_shape=[pltpu.SMEM((8,), jnp.int32), pltpu...  1.18 us
    pallas_call x1, Pallas kernels, local(): pl.pallas_call(join_kernel, out_shape=jax.ShapeDtypeStruct((1, 2 * tokens...  0.99 us
    pallas_call x1, Pallas kernels, local(): pl.pallas_call(begin_kernel, out_shape=[v_buffer, pltpu.VMEM((channels, 3...  0.58 us
  transfers between devices with their start and end apart: 6, of which 0 were waited for; matrix products, arithmetic and copies ran while one was open for 0% of the time, Pallas kernels for 50%

profile of v2, /device:TPU:0, one launch (start us, length us, event | category | flops | bytes accessed | tf_op | source)
XLA Modules:
  0.0 15.7 jit_solution(4359620150375136586)
XLA Ops:
  0.0 3.0 %collective-permute-start = (s32[1,3]{1,0:T(1,128)}, s32[1,3]{1,0:T(1,128)S(1)}, u32[]{:S(2)}, u32[]{:S(2)}) collective-permute-start(s32[1,3]{1,0:T(1,128)} %kind_hbm.1), channel_id=1, source_target_pairs={{0,2},{1,3},{2,0},{3,1},{4,6},{5,7},{6,4},{7,5},{8,10},{9,11},{10,... | collective-permute-start | bytes 44 | tf_op jit(solution)/shard_map/ppermute | solution.py:410
  3.0 1.2 %load.1 = (s32[8]{0:T(128)S(4)}, bf16[256,512]{1,0:T(8,128)(2,1)S(1)}, bf16[80,288]{1,0:T(8,128)(2,1)S(1)}, f32[512]{0:T(512)S(1)}, f32[512]{0:T(512)S(1)}, /*in...) custom-call(s32[1,3]{1,0:T(1,128)} %kind_hbm.1, ...), custom_call_target="tpu_custom_call" | custom-call | bytes 393216 | tf_op jit(solution)/shard_map/load/pallas_call | solution.py:441
  4.2 0.0 slice-start
  4.2 0.0 copy-start
  4.2 0.0 slice-start.1
  4.2 0.6 %begin.1 = (bf16[3,288,512]{2,1,0:T(8,128)(2,1)S(1)}, bf16[512,384]{1,0:T(8,128)(2,1)S(1)}, f32[1,128]{1,0:T(1,128)S(1)}, bf16[64,256]{1,0:T(8,128)(2,1)S(1)}, bf16[80,288]{1,0:T(8,128)(2,1)S(1)}) custom-call(s32[8]{0:T(128)S(4)} %get-tuple-element.25.state_ref, bf16[256,512]{1,0:T(8,128)(2,1)S(1)} %get-tuple-element.26.x_ref, ...), custom_call_target="tpu_custom_call" | custom-call | flops 2491416576 | bytes 393216 | tf_op jit(solution)/shard_map/begin/pallas_call | solution.py:478
  4.8 0.7 %collective-permute-start.3 = (bf16[80,288]{1,0:T(8,128)(2,1)S(1)}, bf16[80,288]{1,0:T(8,128)(2,1)S(1)}, u32[]{:S(2)}, u32[]{:S(2)}) collective-permute-start(bf16[80,288]{1,0:T(8,128)(2,1)S(1)} %get-tuple-element.42.rest_0_), channel_id=1, source_target_pairs={{0,24},{8,16},{16,8},{24,0},{1,25},{9,17},{17,9},{25,1},{2,26},{10... | collective-permute-start | bytes 138248 | tf_op jit(solution)/shard_map/ppermute | solution.py:410
  5.6 0.9 %collective-permute-start.2 = (bf16[80,288]{1,0:T(8,128)(2,1)S(1)}, bf16[80,288]{1,0:T(8,128)(2,1)S(1)}, u32[]{:S(2)}, u32[]{:S(2)}) collective-permute-start(bf16[80,288]{1,0:T(8,128)(2,1)S(1)} %get-tuple-element.42.rest_0_), channel_id=1, source_target_pairs={{0,16},{8,24},{16,0},{24,8},{1,17},{9,25},{17,1},{25,9},{2,18},{10... | collective-permute-start | bytes 138248 | tf_op jit(solution)/shard_map/ppermute | solution.py:410
  6.5 0.3 %collective-permute-start.1 = (bf16[80,288]{1,0:T(8,128)(2,1)S(1)}, bf16[80,288]{1,0:T(8,128)(2,1)S(1)}, u32[]{:S(2)}, u32[]{:S(2)}) collective-permute-start(bf16[80,288]{1,0:T(8,128)(2,1)S(1)} %get-tuple-element.42.rest_0_), channel_id=1, source_target_pairs={{0,8},{8,0},{16,24},{24,16},{1,9},{9,1},{17,25},{25,17},{2,10},{10... | collective-permute-start | bytes 138248 | tf_op jit(solution)/shard_map/ppermute | solution.py:410
  6.8 0.0 collective-permute-done.rest_7_
  6.8 0.0 slice-done
  6.8 0.0 copy-done
  6.8 0.0 slice-done.1
  6.8 3.6 %middle.1 = (bf16[80,128]{1,0:T(8,128)(2,1)S(1)}, s32[1]{0:T(128)S(4)}, bf16[3,288,512]{2,1,0:T(8,128)(2,1)S(1)}) custom-call(s32[8]{0:T(128)S(4)} %get-tuple-element.25.state_ref, bf16[1,768,512]{2,1,0:T(8,128)(2,1)S(1)} %copy-done, bf16[4608,512]{1,0:T(8,128)(2,1)S(1)} %bitcast.2, bf16[64,256]{1,0:T(8,128)(2,1)S(1)} %get-tuple-element.32.perm_ref, ...), custom_call_target="tpu_custom_call" | custom-call | flops 1245708288 | bytes 4718592 | tf_op jit(solution)/shard_map/middle/pallas_call | solution.py:489
  10.4 0.3 %collective-permute-start.5 = (bf16[80,128]{1,0:T(8,128)(2,1)S(1)}, bf16[80,128]{1,0:T(8,128)(2,1)S(1)}, u32[]{:S(2)}, u32[]{:S(2)}) collective-permute-start(bf16[80,128]{1,0:T(8,128)(2,1)S(1)} %get-tuple-element.40.own_ref), channel_id=1, source_target_pairs={{0,8},{7,15},{1,2},{2,1},{3,4},{4,3},{5,6},{6,5},{8,0},{15,7},{9,1... | collective-permute-start | bytes 61448 | tf_op jit(solution)/shard_map/ppermute | solution.py:420
  10.8 1.4 %collective-permute-start.4 = (bf16[80,128]{1,0:T(8,128)(2,1)S(1)}, bf16[80,128]{1,0:T(8,128)(2,1)S(1)}, u32[]{:S(2)}, u32[]{:S(2)}) collective-permute-start(bf16[80,128]{1,0:T(8,128)(2,1)S(1)} %get-tuple-element.40.own_ref), channel_id=1, source_target_pairs={{0,1},{1,0},{2,3},{3,2},{4,5},{5,4},{6,7},{7,6},{8,9},{9,8},{10,11... | collective-permute-start | bytes 61448 | tf_op jit(solution)/shard_map/ppermute | solution.py:410
  12.2 0.0 collective-permute-done.3.rest_3_
  12.2 0.0 collective-permute-done.2.rest_2_
  12.2 0.0 collective-permute-done.1.rest_1_
  12.2 2.5 %final.1 = (bf16[64,64]{1,0:T(8,128)(2,1)S(1)}, bf16[80,1152]{1,0:T(8,128)(2,1)S(1)}) custom-call(s32[8]{0:T(128)S(4)} %get-tuple-element.25.state_ref, bf16[1,768,512]{2,1,0:T(8,128)(2,1)S(1)} %copy-done, bf16[4608,512]{1,0:T(8,128)(2,1)S(1)} %bitcast.2, bf16[64,256]{1,0:T(8,128)(2,1)S(1)} %get-tuple-element.32.perm_ref, ...), custom_call_target="tpu_custom_call" | custom-call | flops 1245708288 | bytes 4718592 | tf_op jit(solution)/shard_map/final/pallas_call | solution.py:503
  14.7 0.0 collective-permute-done.5.odd_ref
  14.7 0.0 collective-permute-done.4.even_ref
  14.7 1.0 %join.1 = bf16[1,128,1152]{2,1,0:T(8,128)(2,1)} custom-call(s32[8]{0:T(128)S(4)} %get-tuple-element.25.state_ref, s32[1]{0:T(128)S(4)} %get-tuple-element.39.sums_ref, bf16[80,128]{1,0:T(8,128)(2,1)S(1)} %get-tuple-element.40.own_ref, bf16[64,64]{1,0:T(8,128)(2,1)S(1)} %get-tuple-element.43.third_ref, bf16[80,128]{1,0:T(8,128)(2,1)S(1)} %collective-permute-done.4.even_ref, ...), custom_call_target="tpu_custom_call" | custom-call | flops 18874368 | bytes 294912 | tf_op jit(solution)/shard_map/join/pallas_call | solution.py:513
  (1 shorter events, 0.0 us)
Async XLA Ops:
  0.0 6.8 %collective-permute-start = (s32[1,3]{1,0:T(1,128)}, s32[1,3]{1,0:T(1,128)S(1)}, u32[]{:S(2)}, u32[]{:S(2)}) collective-permute-start(s32[1,3]{1,0:T(1,128)} %kind_hbm.1), channel_id=1, source_target_pairs={{0,2},{1,3},{2,0},{3,1},{4,6},{5,7},{6,4},{7,5},{8,10},{9,11},{10,... | collective-permute-start | bytes 44 | tf_op jit(solution)/shard_map/ppermute | solution.py:410
  4.2 2.6 %slice-start = ((s8[4718592]{0:T(1024)(128)(4,1)}), s8[4194304]{0:T(1024)(128)(4,1)S(1)}, s32[]{:S(2)}) async-start(s8[4718592]{0:T(1024)(128)(4,1)} %bitcast.1), calls=%async_computation | async-start | bytes 8388608
  4.2 2.5 %copy-start = (bf16[1,768,512]{2,1,0:T(8,128)(2,1)S(1)}, bf16[1,768,512]{2,1,0:T(8,128)(2,1)}, u32[]{:S(2)}) copy-start(bf16[1,768,512]{2,1,0:T(8,128)(2,1)} %x_ref.3) | copy-start | bytes 2359300
  4.2 2.5 %slice-start.1 = ((s8[4718592]{0:T(1024)(128)(4,1)}), s8[524288]{0:T(1024)(128)(4,1)S(1)}, s32[]{:S(2)}) async-start(s8[4718592]{0:T(1024)(128)(4,1)} %bitcast.1), calls=%async_computation.1 | async-start | bytes 1048576
  4.8 7.4 %collective-permute-start.3 = (bf16[80,288]{1,0:T(8,128)(2,1)S(1)}, bf16[80,288]{1,0:T(8,128)(2,1)S(1)}, u32[]{:S(2)}, u32[]{:S(2)}) collective-permute-start(bf16[80,288]{1,0:T(8,128)(2,1)S(1)} %get-tuple-element.42.rest_0_), channel_id=1, source_target_pairs={{0,24},{8,16},{16,8},{24,0},{1,25},{9,17},{17,9},{25,1},{2,26},{10... | collective-permute-start | bytes 138248 | tf_op jit(solution)/shard_map/ppermute | solution.py:410
  5.6 6.6 %collective-permute-start.2 = (bf16[80,288]{1,0:T(8,128)(2,1)S(1)}, bf16[80,288]{1,0:T(8,128)(2,1)S(1)}, u32[]{:S(2)}, u32[]{:S(2)}) collective-permute-start(bf16[80,288]{1,0:T(8,128)(2,1)S(1)} %get-tuple-element.42.rest_0_), channel_id=1, source_target_pairs={{0,16},{8,24},{16,0},{24,8},{1,17},{9,25},{17,1},{25,9},{2,18},{10... | collective-permute-start | bytes 138248 | tf_op jit(solution)/shard_map/ppermute | solution.py:410
  6.5 5.7 %collective-permute-start.1 = (bf16[80,288]{1,0:T(8,128)(2,1)S(1)}, bf16[80,288]{1,0:T(8,128)(2,1)S(1)}, u32[]{:S(2)}, u32[]{:S(2)}) collective-permute-start(bf16[80,288]{1,0:T(8,128)(2,1)S(1)} %get-tuple-element.42.rest_0_), channel_id=1, source_target_pairs={{0,8},{8,0},{16,24},{24,16},{1,9},{9,1},{17,25},{25,17},{2,10},{10... | collective-permute-start | bytes 138248 | tf_op jit(solution)/shard_map/ppermute | solution.py:410
  10.4 4.3 %collective-permute-start.5 = (bf16[80,128]{1,0:T(8,128)(2,1)S(1)}, bf16[80,128]{1,0:T(8,128)(2,1)S(1)}, u32[]{:S(2)}, u32[]{:S(2)}) collective-permute-start(bf16[80,128]{1,0:T(8,128)(2,1)S(1)} %get-tuple-element.40.own_ref), channel_id=1, source_target_pairs={{0,8},{7,15},{1,2},{2,1},{3,4},{4,3},{5,6},{6,5},{8,0},{15,7},{9,1... | collective-permute-start | bytes 61448 | tf_op jit(solution)/shard_map/ppermute | solution.py:420
  10.8 4.0 %collective-permute-start.4 = (bf16[80,128]{1,0:T(8,128)(2,1)S(1)}, bf16[80,128]{1,0:T(8,128)(2,1)S(1)}, u32[]{:S(2)}, u32[]{:S(2)}) collective-permute-start(bf16[80,128]{1,0:T(8,128)(2,1)S(1)} %get-tuple-element.40.own_ref), channel_id=1, source_target_pairs={{0,1},{1,0},{2,3},{3,2},{4,5},{5,4},{6,7},{7,6},{8,9},{9,8},{10,11... | collective-permute-start | bytes 61448 | tf_op jit(solution)/shard_map/ppermute | solution.py:410

commit v3 on v2

--- a/solution.py
+++ b/solution.py
@@ -27,7 +27,9 @@
     rest = packed - high.astype(F32)
     middle = rest.astype(BF16)
     low = (rest - middle.astype(F32)).astype(BF16)
-    total = sum(jnp.dot(piece, same_group, preferred_element_type=F32) for piece in (high, middle, low))
+    total = jnp.dot(jnp.concatenate([high, middle, low], axis=0), same_group, preferred_element_type=F32)
+    size = rows * chunks
+    total = total[:size] + total[size:2 * size] + total[2 * size:]
     return jnp.concatenate([total[k * rows:(k + 1) * rows] for k in range(chunks)], axis=1)
 
 

time: 15.9 us -> 15.8 us (level)
  no operation moved by 1% of the time
where the time goes in v3:
time: 15.8 us; the launch traced here: 15.6 us
  Pallas kernels  8.81 us (56%)
  starting transfers between devices  6.7 us (42%)
    ppermute x5, starting transfers between devices, exchange(): return lax.ppermute(value, axis, [(i, i ^ offset) for i in range(count)])  6.39 us
    pallas_call x1, Pallas kernels, local(): pl.pallas_call(functools.partial(middle_kernel, offsets), out_shape=[jax....  3.62 us
    pallas_call x1, Pallas kernels, local(): pl.pallas_call(functools.partial(final_kernel, dp), out_shape=[pltpu.VMEM...  2.44 us
    pallas_call x1, Pallas kernels, load(): pl.pallas_call(load_kernel, out_shape=[pltpu.SMEM((8,), jnp.int32), pltpu...  1.18 us
    pallas_call x1, Pallas kernels, local(): pl.pallas_call(join_kernel, out_shape=jax.ShapeDtypeStruct((1, 2 * tokens...  0.99 us
    pallas_call x1, Pallas kernels, local(): pl.pallas_call(begin_kernel, out_shape=[v_buffer, pltpu.VMEM((channels, 3...  0.58 us
  transfers between devices with their start and end apart: 6, of which 0 were waited for; matrix products, arithmetic and copies ran while one was open for 0% of the time, Pallas kernels for 50%

profile of v3, /device:TPU:0, one launch (start us, length us, event | category | flops | bytes accessed | tf_op | source)
XLA Modules:
  0.0 15.6 jit_solution(10501474887522393767)
XLA Ops:
  0.0 3.0 %collective-permute-start = (s32[1,3]{1,0:T(1,128)}, s32[1,3]{1,0:T(1,128)S(1)}, u32[]{:S(2)}, u32[]{:S(2)}) collective-permute-start(s32[1,3]{1,0:T(1,128)} %kind_hbm.1), channel_id=1, source_target_pairs={{0,2},{1,3},{2,0},{3,1},{4,6},{5,7},{6,4},{7,5},{8,10},{9,11},{10,... | collective-permute-start | bytes 44 | tf_op jit(solution)/shard_map/ppermute | solution.py:412
  3.0 1.2 %load.1 = (s32[8]{0:T(128)S(4)}, bf16[256,512]{1,0:T(8,128)(2,1)S(1)}, bf16[80,288]{1,0:T(8,128)(2,1)S(1)}, f32[512]{0:T(512)S(1)}, f32[512]{0:T(512)S(1)}, /*in...) custom-call(s32[1,3]{1,0:T(1,128)} %kind_hbm.1, ...), custom_call_target="tpu_custom_call" | custom-call | bytes 393216 | tf_op jit(solution)/shard_map/load/pallas_call | solution.py:443
  4.2 0.0 slice-start
  4.2 0.0 copy-start
  4.2 0.0 slice-start.1
  4.2 0.6 %begin.1 = (bf16[3,288,512]{2,1,0:T(8,128)(2,1)S(1)}, bf16[512,384]{1,0:T(8,128)(2,1)S(1)}, f32[1,128]{1,0:T(1,128)S(1)}, bf16[64,256]{1,0:T(8,128)(2,1)S(1)}, bf16[80,288]{1,0:T(8,128)(2,1)S(1)}) custom-call(s32[8]{0:T(128)S(4)} %get-tuple-element.25.state_ref, bf16[256,512]{1,0:T(8,128)(2,1)S(1)} %get-tuple-element.26.x_ref, ...), custom_call_target="tpu_custom_call" | custom-call | flops 2491416576 | bytes 393216 | tf_op jit(solution)/shard_map/begin/pallas_call | solution.py:480
  4.8 0.7 %collective-permute-start.3 = (bf16[80,288]{1,0:T(8,128)(2,1)S(1)}, bf16[80,288]{1,0:T(8,128)(2,1)S(1)}, u32[]{:S(2)}, u32[]{:S(2)}) collective-permute-start(bf16[80,288]{1,0:T(8,128)(2,1)S(1)} %get-tuple-element.42.rest_0_), channel_id=1, source_target_pairs={{0,24},{8,16},{16,8},{24,0},{1,25},{9,17},{17,9},{25,1},{2,26},{10... | collective-permute-start | bytes 138248 | tf_op jit(solution)/shard_map/ppermute | solution.py:412
  5.6 0.9 %collective-permute-start.2 = (bf16[80,288]{1,0:T(8,128)(2,1)S(1)}, bf16[80,288]{1,0:T(8,128)(2,1)S(1)}, u32[]{:S(2)}, u32[]{:S(2)}) collective-permute-start(bf16[80,288]{1,0:T(8,128)(2,1)S(1)} %get-tuple-element.42.rest_0_), channel_id=1, source_target_pairs={{0,16},{8,24},{16,0},{24,8},{1,17},{9,25},{17,1},{25,9},{2,18},{10... | collective-permute-start | bytes 138248 | tf_op jit(solution)/shard_map/ppermute | solution.py:412
  6.5 0.3 %collective-permute-start.1 = (bf16[80,288]{1,0:T(8,128)(2,1)S(1)}, bf16[80,288]{1,0:T(8,128)(2,1)S(1)}, u32[]{:S(2)}, u32[]{:S(2)}) collective-permute-start(bf16[80,288]{1,0:T(8,128)(2,1)S(1)} %get-tuple-element.42.rest_0_), channel_id=1, source_target_pairs={{0,8},{8,0},{16,24},{24,16},{1,9},{9,1},{17,25},{25,17},{2,10},{10... | collective-permute-start | bytes 138248 | tf_op jit(solution)/shard_map/ppermute | solution.py:412
  6.8 0.0 collective-permute-done.rest_7_
  6.8 0.0 slice-done
  6.8 0.0 copy-done
  6.8 0.0 slice-done.1
  6.8 3.6 %middle.1 = (bf16[80,128]{1,0:T(8,128)(2,1)S(1)}, s32[1]{0:T(128)S(4)}, bf16[3,288,512]{2,1,0:T(8,128)(2,1)S(1)}) custom-call(s32[8]{0:T(128)S(4)} %get-tuple-element.25.state_ref, bf16[1,768,512]{2,1,0:T(8,128)(2,1)S(1)} %copy-done, bf16[4608,512]{1,0:T(8,128)(2,1)S(1)} %bitcast.2, bf16[64,256]{1,0:T(8,128)(2,1)S(1)} %get-tuple-element.32.perm_ref, ...), custom_call_target="tpu_custom_call" | custom-call | flops 1245708288 | bytes 4718592 | tf_op jit(solution)/shard_map/middle/pallas_call | solution.py:491
  10.4 0.3 %collective-permute-start.5 = (bf16[80,128]{1,0:T(8,128)(2,1)S(1)}, bf16[80,128]{1,0:T(8,128)(2,1)S(1)}, u32[]{:S(2)}, u32[]{:S(2)}) collective-permute-start(bf16[80,128]{1,0:T(8,128)(2,1)S(1)} %get-tuple-element.40.own_ref), channel_id=1, source_target_pairs={{0,8},{7,15},{1,2},{2,1},{3,4},{4,3},{5,6},{6,5},{8,0},{15,7},{9,1... | collective-permute-start | bytes 61448 | tf_op jit(solution)/shard_map/ppermute | solution.py:422
  10.7 1.4 %collective-permute-start.4 = (bf16[80,128]{1,0:T(8,128)(2,1)S(1)}, bf16[80,128]{1,0:T(8,128)(2,1)S(1)}, u32[]{:S(2)}, u32[]{:S(2)}) collective-permute-start(bf16[80,128]{1,0:T(8,128)(2,1)S(1)} %get-tuple-element.40.own_ref), channel_id=1, source_target_pairs={{0,1},{1,0},{2,3},{3,2},{4,5},{5,4},{6,7},{7,6},{8,9},{9,8},{10,11... | collective-permute-start | bytes 61448 | tf_op jit(solution)/shard_map/ppermute | solution.py:412
  12.2 0.0 collective-permute-done.3.rest_3_
  12.2 0.0 collective-permute-done.2.rest_2_
  12.2 0.0 collective-permute-done.1.rest_1_
  12.2 2.4 %final.1 = (bf16[64,64]{1,0:T(8,128)(2,1)S(1)}, bf16[80,1152]{1,0:T(8,128)(2,1)S(1)}) custom-call(s32[8]{0:T(128)S(4)} %get-tuple-element.25.state_ref, bf16[1,768,512]{2,1,0:T(8,128)(2,1)S(1)} %copy-done, bf16[4608,512]{1,0:T(8,128)(2,1)S(1)} %bitcast.2, bf16[64,256]{1,0:T(8,128)(2,1)S(1)} %get-tuple-element.32.perm_ref, ...), custom_call_target="tpu_custom_call" | custom-call | flops 1245708288 | bytes 4718592 | tf_op jit(solution)/shard_map/final/pallas_call | solution.py:505
  14.6 0.0 collective-permute-done.5.odd_ref
  14.6 0.0 collective-permute-done.4.even_ref
  14.6 1.0 %join.1 = bf16[1,128,1152]{2,1,0:T(8,128)(2,1)} custom-call(s32[8]{0:T(128)S(4)} %get-tuple-element.25.state_ref, s32[1]{0:T(128)S(4)} %get-tuple-element.39.sums_ref, bf16[80,128]{1,0:T(8,128)(2,1)S(1)} %get-tuple-element.40.own_ref, bf16[64,64]{1,0:T(8,128)(2,1)S(1)} %get-tuple-element.43.third_ref, bf16[80,128]{1,0:T(8,128)(2,1)S(1)} %collective-permute-done.4.even_ref, ...), custom_call_target="tpu_custom_call" | custom-call | flops 18874368 | bytes 294912 | tf_op jit(solution)/shard_map/join/pallas_call | solution.py:515
  (1 shorter events, 0.0 us)
Async XLA Ops:
  0.0 6.8 %collective-permute-start = (s32[1,3]{1,0:T(1,128)}, s32[1,3]{1,0:T(1,128)S(1)}, u32[]{:S(2)}, u32[]{:S(2)}) collective-permute-start(s32[1,3]{1,0:T(1,128)} %kind_hbm.1), channel_id=1, source_target_pairs={{0,2},{1,3},{2,0},{3,1},{4,6},{5,7},{6,4},{7,5},{8,10},{9,11},{10,... | collective-permute-start | bytes 44 | tf_op jit(solution)/shard_map/ppermute | solution.py:412
  4.2 2.6 %slice-start = ((s8[4718592]{0:T(1024)(128)(4,1)}), s8[4194304]{0:T(1024)(128)(4,1)S(1)}, s32[]{:S(2)}) async-start(s8[4718592]{0:T(1024)(128)(4,1)} %bitcast.1), calls=%async_computation | async-start | bytes 8388608
  4.2 2.5 %copy-start = (bf16[1,768,512]{2,1,0:T(8,128)(2,1)S(1)}, bf16[1,768,512]{2,1,0:T(8,128)(2,1)}, u32[]{:S(2)}) copy-start(bf16[1,768,512]{2,1,0:T(8,128)(2,1)} %x_ref.3) | copy-start | bytes 2359300
  4.2 2.5 %slice-start.1 = ((s8[4718592]{0:T(1024)(128)(4,1)}), s8[524288]{0:T(1024)(128)(4,1)S(1)}, s32[]{:S(2)}) async-start(s8[4718592]{0:T(1024)(128)(4,1)} %bitcast.1), calls=%async_computation.1 | async-start | bytes 1048576
  4.8 7.3 %collective-permute-start.3 = (bf16[80,288]{1,0:T(8,128)(2,1)S(1)}, bf16[80,288]{1,0:T(8,128)(2,1)S(1)}, u32[]{:S(2)}, u32[]{:S(2)}) collective-permute-start(bf16[80,288]{1,0:T(8,128)(2,1)S(1)} %get-tuple-element.42.rest_0_), channel_id=1, source_target_pairs={{0,24},{8,16},{16,8},{24,0},{1,25},{9,17},{17,9},{25,1},{2,26},{10... | collective-permute-start | bytes 138248 | tf_op jit(solution)/shard_map/ppermute | solution.py:412
  5.6 6.6 %collective-permute-start.2 = (bf16[80,288]{1,0:T(8,128)(2,1)S(1)}, bf16[80,288]{1,0:T(8,128)(2,1)S(1)}, u32[]{:S(2)}, u32[]{:S(2)}) collective-permute-start(bf16[80,288]{1,0:T(8,128)(2,1)S(1)} %get-tuple-element.42.rest_0_), channel_id=1, source_target_pairs={{0,16},{8,24},{16,0},{24,8},{1,17},{9,25},{17,1},{25,9},{2,18},{10... | collective-permute-start | bytes 138248 | tf_op jit(solution)/shard_map/ppermute | solution.py:412
  6.5 5.7 %collective-permute-start.1 = (bf16[80,288]{1,0:T(8,128)(2,1)S(1)}, bf16[80,288]{1,0:T(8,128)(2,1)S(1)}, u32[]{:S(2)}, u32[]{:S(2)}) collective-permute-start(bf16[80,288]{1,0:T(8,128)(2,1)S(1)} %get-tuple-element.42.rest_0_), channel_id=1, source_target_pairs={{0,8},{8,0},{16,24},{24,16},{1,9},{9,1},{17,25},{25,17},{2,10},{10... | collective-permute-start | bytes 138248 | tf_op jit(solution)/shard_map/ppermute | solution.py:412
  10.4 4.2 %collective-permute-start.5 = (bf16[80,128]{1,0:T(8,128)(2,1)S(1)}, bf16[80,128]{1,0:T(8,128)(2,1)S(1)}, u32[]{:S(2)}, u32[]{:S(2)}) collective-permute-start(bf16[80,128]{1,0:T(8,128)(2,1)S(1)} %get-tuple-element.40.own_ref), channel_id=1, source_target_pairs={{0,8},{7,15},{1,2},{2,1},{3,4},{4,3},{5,6},{6,5},{8,0},{15,7},{9,1... | collective-permute-start | bytes 61448 | tf_op jit(solution)/shard_map/ppermute | solution.py:422
  10.7 3.9 %collective-permute-start.4 = (bf16[80,128]{1,0:T(8,128)(2,1)S(1)}, bf16[80,128]{1,0:T(8,128)(2,1)S(1)}, u32[]{:S(2)}, u32[]{:S(2)}) collective-permute-start(bf16[80,128]{1,0:T(8,128)(2,1)S(1)} %get-tuple-element.40.own_ref), channel_id=1, source_target_pairs={{0,1},{1,0},{2,3},{3,2},{4,5},{5,4},{6,7},{7,6},{8,9},{9,8},{10,11... | collective-permute-start | bytes 61448 | tf_op jit(solution)/shard_map/ppermute | solution.py:412

commit v4 on v3

--- a/solution.py
+++ b/solution.py
@@ -90,7 +90,7 @@
         yield
 
 
-def conv_steps(x_ref, bias, w_ref, v_ref, y_ref):
+def conv_steps(x_ref, bias, w_ref, v_ref, y_ref, by_half=False):
     cells, channels = x_ref.shape
     half = cells // 2
     tile = channels // 2
@@ -99,7 +99,16 @@
         lanes = slice(k * tile, (k + 1) * tile)
         x = x_ref[:, lanes].astype(F32).reshape(2, half // SLOT_COLS, SLOT_COLS, tile)
         totals.append(halves_together(x[0], x[1]).reshape(cells, tile) + bias[:, lanes])
-    for a in range(3):
+    for deep in [slice(h * tile, (h + 1) * tile) for h in range(2)] if by_half else []:
+        for a in range(3):
+            rows = slice(2 * SLOT_COLS * a, 2 * SLOT_COLS * a + cells)
+            lhs = jnp.concatenate([v_ref[b, rows, deep] for b in range(3)], axis=1)
+            for k in range(2):
+                weight = jnp.concatenate([w_ref[(3 * a + b) * channels + deep.start:(3 * a + b) * channels + deep.stop,
+                                                k * tile:(k + 1) * tile] for b in range(3)], axis=0)
+                totals[k] = totals[k] + jnp.dot(lhs, weight, preferred_element_type=F32)
+                yield
+    for a in range(0 if by_half else 3):
         for b in range(3):
             lhs = v_ref[b, 2 * SLOT_COLS * a:2 * SLOT_COLS * a + cells, :]
             base = (3 * a + b) * channels
@@ -369,9 +378,10 @@
             out_ref[...] = value
 
         x = x_ref.at[0, 0:y_ref.shape[0], :]
-        interleave(norm_first_steps(x, state_ref[2] == 2, vector(small[0]), vector(small[1]),
-                                    group_table(y_ref.shape[1]), v_ref), lay_out())
-        drain(conv_steps(x, vector(small[2]), w_ref, v_ref, y_ref))
+        norm = norm_first_steps(x, state_ref[2] == 2, vector(small[0]), vector(small[1]), group_table(y_ref.shape[1]), v_ref)
+        for _ in range(6):
+            next(norm)
+        interleave(conv_steps(x, vector(small[2]), w_ref, v_ref, y_ref, by_half=True), norm, lay_out())
         drain(second_norm(y_ref, state_ref[2], small))
         drain(patches(store, y_ref, state_ref[2], small, perm_ref))
 

time: 15.8 us -> 15.8 us (level)
  no operation moved by 1% of the time
where the time goes in v4:
time: 15.8 us; the launch traced here: 15.6 us
  Pallas kernels  8.79 us (56%)
  starting transfers between devices  6.7 us (42%)
    ppermute x5, starting transfers between devices, exchange(): return lax.ppermute(value, axis, [(i, i ^ offset) for i in range(count)])  6.39 us
    pallas_call x1, Pallas kernels, local(): pl.pallas_call(functools.partial(middle_kernel, offsets), out_shape=[jax....  3.62 us
    pallas_call x1, Pallas kernels, local(): pl.pallas_call(functools.partial(final_kernel, dp), out_shape=[pltpu.VMEM...  2.42 us
    pallas_call x1, Pallas kernels, load(): pl.pallas_call(load_kernel, out_shape=[pltpu.SMEM((8,), jnp.int32), pltpu...  1.18 us
    pallas_call x1, Pallas kernels, local(): pl.pallas_call(join_kernel, out_shape=jax.ShapeDtypeStruct((1, 2 * tokens...  0.99 us
    pallas_call x1, Pallas kernels, local(): pl.pallas_call(begin_kernel, out_shape=[v_buffer, pltpu.VMEM((channels, 3...  0.58 us
  transfers between devices with their start and end apart: 6, of which 0 were waited for; matrix products, arithmetic and copies ran while one was open for 0% of the time, Pallas kernels for 50%

profile of v4, /device:TPU:0, one launch (start us, length us, event | category | flops | bytes accessed | tf_op | source)
XLA Modules:
  0.0 15.6 jit_solution(18028170805116308011)
XLA Ops:
  0.0 3.0 %collective-permute-start = (s32[1,3]{1,0:T(1,128)}, s32[1,3]{1,0:T(1,128)S(1)}, u32[]{:S(2)}, u32[]{:S(2)}) collective-permute-start(s32[1,3]{1,0:T(1,128)} %kind_hbm.1), channel_id=1, source_target_pairs={{0,2},{1,3},{2,0},{3,1},{4,6},{5,7},{6,4},{7,5},{8,10},{9,11},{10,... | collective-permute-start | bytes 44 | tf_op jit(solution)/shard_map/ppermute | solution.py:422
  3.0 1.2 %load.1 = (s32[8]{0:T(128)S(4)}, bf16[256,512]{1,0:T(8,128)(2,1)S(1)}, bf16[80,288]{1,0:T(8,128)(2,1)S(1)}, f32[512]{0:T(512)S(1)}, f32[512]{0:T(512)S(1)}, /*in...) custom-call(s32[1,3]{1,0:T(1,128)} %kind_hbm.1, ...), custom_call_target="tpu_custom_call" | custom-call | bytes 393216 | tf_op jit(solution)/shard_map/load/pallas_call | solution.py:453
  4.2 0.0 slice-start
  4.2 0.0 copy-start
  4.2 0.0 slice-start.1
  4.2 0.6 %begin.1 = (bf16[3,288,512]{2,1,0:T(8,128)(2,1)S(1)}, bf16[512,384]{1,0:T(8,128)(2,1)S(1)}, f32[1,128]{1,0:T(1,128)S(1)}, bf16[64,256]{1,0:T(8,128)(2,1)S(1)}, bf16[80,288]{1,0:T(8,128)(2,1)S(1)}) custom-call(s32[8]{0:T(128)S(4)} %get-tuple-element.25.state_ref, bf16[256,512]{1,0:T(8,128)(2,1)S(1)} %get-tuple-element.26.x_ref, ...), custom_call_target="tpu_custom_call" | custom-call | flops 2491416576 | bytes 393216 | tf_op jit(solution)/shard_map/begin/pallas_call | solution.py:490
  4.8 0.7 %collective-permute-start.3 = (bf16[80,288]{1,0:T(8,128)(2,1)S(1)}, bf16[80,288]{1,0:T(8,128)(2,1)S(1)}, u32[]{:S(2)}, u32[]{:S(2)}) collective-permute-start(bf16[80,288]{1,0:T(8,128)(2,1)S(1)} %get-tuple-element.42.rest_0_), channel_id=1, source_target_pairs={{0,24},{8,16},{16,8},{24,0},{1,25},{9,17},{17,9},{25,1},{2,26},{10... | collective-permute-start | bytes 138248 | tf_op jit(solution)/shard_map/ppermute | solution.py:422
  5.6 0.9 %collective-permute-start.2 = (bf16[80,288]{1,0:T(8,128)(2,1)S(1)}, bf16[80,288]{1,0:T(8,128)(2,1)S(1)}, u32[]{:S(2)}, u32[]{:S(2)}) collective-permute-start(bf16[80,288]{1,0:T(8,128)(2,1)S(1)} %get-tuple-element.42.rest_0_), channel_id=1, source_target_pairs={{0,16},{8,24},{16,0},{24,8},{1,17},{9,25},{17,1},{25,9},{2,18},{10... | collective-permute-start | bytes 138248 | tf_op jit(solution)/shard_map/ppermute | solution.py:422
  6.5 0.3 %collective-permute-start.1 = (bf16[80,288]{1,0:T(8,128)(2,1)S(1)}, bf16[80,288]{1,0:T(8,128)(2,1)S(1)}, u32[]{:S(2)}, u32[]{:S(2)}) collective-permute-start(bf16[80,288]{1,0:T(8,128)(2,1)S(1)} %get-tuple-element.42.rest_0_), channel_id=1, source_target_pairs={{0,8},{8,0},{16,24},{24,16},{1,9},{9,1},{17,25},{25,17},{2,10},{10... | collective-permute-start | bytes 138248 | tf_op jit(solution)/shard_map/ppermute | solution.py:422
  6.8 0.0 collective-permute-done.rest_7_
  6.8 0.0 slice-done
  6.8 0.0 copy-done
  6.8 0.0 slice-done.1
  6.8 3.6 %middle.1 = (bf16[80,128]{1,0:T(8,128)(2,1)S(1)}, s32[1]{0:T(128)S(4)}, bf16[3,288,512]{2,1,0:T(8,128)(2,1)S(1)}) custom-call(s32[8]{0:T(128)S(4)} %get-tuple-element.25.state_ref, bf16[1,768,512]{2,1,0:T(8,128)(2,1)S(1)} %copy-done, bf16[4608,512]{1,0:T(8,128)(2,1)S(1)} %bitcast.2, bf16[64,256]{1,0:T(8,128)(2,1)S(1)} %get-tuple-element.32.perm_ref, ...), custom_call_target="tpu_custom_call" | custom-call | flops 1245708288 | bytes 4718592 | tf_op jit(solution)/shard_map/middle/pallas_call | solution.py:501
  10.4 0.3 %collective-permute-start.5 = (bf16[80,128]{1,0:T(8,128)(2,1)S(1)}, bf16[80,128]{1,0:T(8,128)(2,1)S(1)}, u32[]{:S(2)}, u32[]{:S(2)}) collective-permute-start(bf16[80,128]{1,0:T(8,128)(2,1)S(1)} %get-tuple-element.40.own_ref), channel_id=1, source_target_pairs={{0,8},{7,15},{1,2},{2,1},{3,4},{4,3},{5,6},{6,5},{8,0},{15,7},{9,1... | collective-permute-start | bytes 61448 | tf_op jit(solution)/shard_map/ppermute | solution.py:432
  10.7 1.4 %collective-permute-start.4 = (bf16[80,128]{1,0:T(8,128)(2,1)S(1)}, bf16[80,128]{1,0:T(8,128)(2,1)S(1)}, u32[]{:S(2)}, u32[]{:S(2)}) collective-permute-start(bf16[80,128]{1,0:T(8,128)(2,1)S(1)} %get-tuple-element.40.own_ref), channel_id=1, source_target_pairs={{0,1},{1,0},{2,3},{3,2},{4,5},{5,4},{6,7},{7,6},{8,9},{9,8},{10,11... | collective-permute-start | bytes 61448 | tf_op jit(solution)/shard_map/ppermute | solution.py:422
  12.2 0.0 collective-permute-done.3.rest_3_
  12.2 0.0 collective-permute-done.2.rest_2_
  12.2 0.0 collective-permute-done.1.rest_1_
  12.2 2.4 %final.1 = (bf16[64,64]{1,0:T(8,128)(2,1)S(1)}, bf16[80,1152]{1,0:T(8,128)(2,1)S(1)}) custom-call(s32[8]{0:T(128)S(4)} %get-tuple-element.25.state_ref, bf16[1,768,512]{2,1,0:T(8,128)(2,1)S(1)} %copy-done, bf16[4608,512]{1,0:T(8,128)(2,1)S(1)} %bitcast.2, bf16[64,256]{1,0:T(8,128)(2,1)S(1)} %get-tuple-element.32.perm_ref, ...), custom_call_target="tpu_custom_call" | custom-call | flops 1245708288 | bytes 4718592 | tf_op jit(solution)/shard_map/final/pallas_call | solution.py:515
  14.6 0.0 collective-permute-done.5.odd_ref
  14.6 0.0 collective-permute-done.4.even_ref
  14.6 1.0 %join.1 = bf16[1,128,1152]{2,1,0:T(8,128)(2,1)} custom-call(s32[8]{0:T(128)S(4)} %get-tuple-element.25.state_ref, s32[1]{0:T(128)S(4)} %get-tuple-element.39.sums_ref, bf16[80,128]{1,0:T(8,128)(2,1)S(1)} %get-tuple-element.40.own_ref, bf16[64,64]{1,0:T(8,128)(2,1)S(1)} %get-tuple-element.43.third_ref, bf16[80,128]{1,0:T(8,128)(2,1)S(1)} %collective-permute-done.4.even_ref, ...), custom_call_target="tpu_custom_call" | custom-call | flops 18874368 | bytes 294912 | tf_op jit(solution)/shard_map/join/pallas_call | solution.py:525
  (1 shorter events, 0.0 us)
Async XLA Ops:
  0.0 6.8 %collective-permute-start = (s32[1,3]{1,0:T(1,128)}, s32[1,3]{1,0:T(1,128)S(1)}, u32[]{:S(2)}, u32[]{:S(2)}) collective-permute-start(s32[1,3]{1,0:T(1,128)} %kind_hbm.1), channel_id=1, source_target_pairs={{0,2},{1,3},{2,0},{3,1},{4,6},{5,7},{6,4},{7,5},{8,10},{9,11},{10,... | collective-permute-start | bytes 44 | tf_op jit(solution)/shard_map/ppermute | solution.py:422
  4.2 2.6 %slice-start = ((s8[4718592]{0:T(1024)(128)(4,1)}), s8[4194304]{0:T(1024)(128)(4,1)S(1)}, s32[]{:S(2)}) async-start(s8[4718592]{0:T(1024)(128)(4,1)} %bitcast.1), calls=%async_computation | async-start | bytes 8388608
  4.2 2.5 %copy-start = (bf16[1,768,512]{2,1,0:T(8,128)(2,1)S(1)}, bf16[1,768,512]{2,1,0:T(8,128)(2,1)}, u32[]{:S(2)}) copy-start(bf16[1,768,512]{2,1,0:T(8,128)(2,1)} %x_ref.3) | copy-start | bytes 2359300
  4.2 2.5 %slice-start.1 = ((s8[4718592]{0:T(1024)(128)(4,1)}), s8[524288]{0:T(1024)(128)(4,1)S(1)}, s32[]{:S(2)}) async-start(s8[4718592]{0:T(1024)(128)(4,1)} %bitcast.1), calls=%async_computation.1 | async-start | bytes 1048576
  4.8 7.3 %collective-permute-start.3 = (bf16[80,288]{1,0:T(8,128)(2,1)S(1)}, bf16[80,288]{1,0:T(8,128)(2,1)S(1)}, u32[]{:S(2)}, u32[]{:S(2)}) collective-permute-start(bf16[80,288]{1,0:T(8,128)(2,1)S(1)} %get-tuple-element.42.rest_0_), channel_id=1, source_target_pairs={{0,24},{8,16},{16,8},{24,0},{1,25},{9,17},{17,9},{25,1},{2,26},{10... | collective-permute-start | bytes 138248 | tf_op jit(solution)/shard_map/ppermute | solution.py:422
  5.6 6.6 %collective-permute-start.2 = (bf16[80,288]{1,0:T(8,128)(2,1)S(1)}, bf16[80,288]{1,0:T(8,128)(2,1)S(1)}, u32[]{:S(2)}, u32[]{:S(2)}) collective-permute-start(bf16[80,288]{1,0:T(8,128)(2,1)S(1)} %get-tuple-element.42.rest_0_), channel_id=1, source_target_pairs={{0,16},{8,24},{16,0},{24,8},{1,17},{9,25},{17,1},{25,9},{2,18},{10... | collective-permute-start | bytes 138248 | tf_op jit(solution)/shard_map/ppermute | solution.py:422
  6.5 5.7 %collective-permute-start.1 = (bf16[80,288]{1,0:T(8,128)(2,1)S(1)}, bf16[80,288]{1,0:T(8,128)(2,1)S(1)}, u32[]{:S(2)}, u32[]{:S(2)}) collective-permute-start(bf16[80,288]{1,0:T(8,128)(2,1)S(1)} %get-tuple-element.42.rest_0_), channel_id=1, source_target_pairs={{0,8},{8,0},{16,24},{24,16},{1,9},{9,1},{17,25},{25,17},{2,10},{10... | collective-permute-start | bytes 138248 | tf_op jit(solution)/shard_map/ppermute | solution.py:422
  10.4 4.2 %collective-permute-start.5 = (bf16[80,128]{1,0:T(8,128)(2,1)S(1)}, bf16[80,128]{1,0:T(8,128)(2,1)S(1)}, u32[]{:S(2)}, u32[]{:S(2)}) collective-permute-start(bf16[80,128]{1,0:T(8,128)(2,1)S(1)} %get-tuple-element.40.own_ref), channel_id=1, source_target_pairs={{0,8},{7,15},{1,2},{2,1},{3,4},{4,3},{5,6},{6,5},{8,0},{15,7},{9,1... | collective-permute-start | bytes 61448 | tf_op jit(solution)/shard_map/ppermute | solution.py:432
  10.7 3.9 %collective-permute-start.4 = (bf16[80,128]{1,0:T(8,128)(2,1)S(1)}, bf16[80,128]{1,0:T(8,128)(2,1)S(1)}, u32[]{:S(2)}, u32[]{:S(2)}) collective-permute-start(bf16[80,128]{1,0:T(8,128)(2,1)S(1)} %get-tuple-element.40.own_ref), channel_id=1, source_target_pairs={{0,1},{1,0},{2,3},{3,2},{4,5},{5,4},{6,7},{7,6},{8,9},{9,8},{10,11... | collective-permute-start | bytes 61448 | tf_op jit(solution)/shard_map/ppermute | solution.py:422
